TPU v7x, 512 devices: a whole 4x4x16 slice. The times are simulated.
512 devices in a mesh: gx: 16 (over y, z_hi, core), gy: 8 (over z_lo), vert: 4 (over x).
Axes of the slice: x: 4, y: 4, z: 16 (z_hi: 2, z_lo: 8; z = z_hi * 8 + z_lo), core: 2. Of those that a mesh axis runs over, the one named last changes fastest.
Arguments:
- distribution: float32 [64, 16, 13824], P('gx', 'gy', 'vert'), may hold values from 0.1 to 1
- cell_types: int32 [64, 16], P('gx', 'gy'), may hold values from 0 to 2, as said below
- wall_state: float32 [13824], P('vert'), may hold values from 0.1 to 1
- inflow_state: float32 [13824], P('vert'), may hold values from 0.05 to 1.2
- upwind_side: int32 [2, 13824], P(None, 'vert'), may hold values from 0 to 1
- gain_left: float32 [4, 24, 24, 24], replicated, may hold values from -2 to 2
- gain_right: float32 [4, 24, 24, 24], replicated, may hold values from -2 to 2
- loss_table: float32 [24, 24, 24], replicated, may hold values from 0.5 to 1.5
Outputs:
- advanced: float32 [64, 16, 13824], P('gx', 'gy', 'vert')
Inputs may be any that keep to these rules, and one draw needn't show every extreme that they name: `cell_types`: row y = 0 is wall; along every streamwise position x the cells from some wall-normal index up to y = 15 are wall (between 1 and 5 rows, varying with x); the gas cells at x = 0 are inflow; all other cells are gas.
All inputs are finite; a program needn't handle non-finite values.
Results may differ from a plain program's by a relative error of at most 0.0001.
Values sent between devices are 32-bit elements; how exact they have to be, the bound alone decides.
A program may use at most 64 MiB of HBM per device.

v0:
```python
import jax
import jax.numpy as jnp
from jax import lax
from jax.sharding import PartitionSpec as P

collision_step = 0.25
courant = 0.45
highest = lax.Precision.HIGHEST


def padded_2(shard, sides, width):
    for axis, dim in sides:
        peers, length = (lax.axis_size(axis), shard.shape[dim])
        up = [(i, (i + 1) % peers) for i in range(peers - 1)]
        down = [(j, i) for i, j in up]
        last = lax.slice_in_dim(shard, length - width, length, axis=dim)
        leading = lax.slice_in_dim(shard, 0, width, axis=dim)
        before = lax.ppermute(last, axis, up)
        after = lax.ppermute(leading, axis, down)
        shard = jnp.concatenate([before, shard, after], axis=dim)
    return shard


def twiddles(size_v):
    indices = jnp.arange(size_v, dtype=jnp.int32)
    phases = (
        2.0 * jnp.pi / size_v * (indices[:, None] * indices[None, :] % size_v).astype(jnp.float32)
    )
    cosine = jnp.cos(phases)
    sine_table = jnp.sin(phases)
    forward = jnp.stack(
        [jnp.stack([cosine, sine_table], 1), jnp.stack([-sine_table, cosine], 1)], 0
    )
    inverse = (
        jnp.stack([jnp.stack([cosine, -sine_table], 1), jnp.stack([sine_table, cosine], 1)], 0)
        / size_v
    )
    plane_size = size_v * size_v
    flat = jnp.arange(plane_size, dtype=jnp.int32)
    first = flat // size_v
    second = flat % size_v
    products = (first[:, None] * first[None, :] + second[:, None] * second[None, :]) % size_v
    plane_phases = 2.0 * jnp.pi / size_v * products.astype(jnp.float32)
    plane_cos = jnp.cos(plane_phases)
    plane_sin = jnp.sin(plane_phases)
    plane_forward = jnp.stack([plane_cos, -plane_sin], 1)
    plane_inverse = jnp.stack([plane_cos, -plane_sin], 0) / plane_size
    return (forward, inverse, plane_forward, plane_inverse)


def collide_cell(cell_block, multipliers, rank_count, tables):
    forward, inverse, plane_forward, plane_inverse = tables
    half = jnp.einsum("xj,jpk->pxk", cell_block, plane_forward, precision=highest)
    spectrum = jnp.einsum("pkqj,qjz->pkz", forward, half, precision=highest)
    shaped = spectrum[None] * multipliers[:, None]
    shaped = jnp.einsum("pkqj,tqjz->tpkz", inverse, shaped, precision=highest)
    fields = jnp.einsum("tqxj,qjk->txk", shaped, plane_inverse, precision=highest)
    gain_sum = jnp.sum(fields[:rank_count] * fields[rank_count : 2 * rank_count], axis=0)
    loss_rate = fields[2 * rank_count]
    return cell_block + collision_step * (gain_sum - cell_block * loss_rate)


def transport(padded, upwind_side, plane_start, size_v):
    velocities = padded.shape[2]
    velocity_index = jnp.arange(velocities, dtype=jnp.int32)
    plane_index = velocity_index // (size_v * size_v) + plane_start
    column_index = velocity_index // size_v % size_v
    courant_x = courant * jnp.abs(2 * plane_index - (size_v - 1)).astype(jnp.float32) / (size_v - 1)
    courant_y = (
        courant * jnp.abs(2 * column_index - (size_v - 1)).astype(jnp.float32) / (size_v - 1)
    )
    centre = padded[1:-1, 1:-1]
    upstream_x = jnp.where(upwind_side[0] == 1, padded[:-2, 1:-1], padded[2:, 1:-1])
    upstream_y = jnp.where(upwind_side[1] == 1, padded[1:-1, :-2], padded[1:-1, 2:])
    return centre - courant_x * (centre - upstream_x) - courant_y * (centre - upstream_y)


def on_device(
    distribution,
    cell_types,
    wall_state,
    inflow_state,
    upwind_side,
    gain_left,
    gain_right,
    loss_table,
):
    size_v = loss_table.shape[0]
    rank_count = gain_left.shape[0]
    plane_size = size_v * size_v
    groups = lax.axis_size("vert")
    planes = distribution.shape[2] // plane_size
    kind_column = cell_types[:, :, None]
    boundary_state = jnp.where(
        kind_column == 1,
        wall_state[None, None, :],
        jnp.where(kind_column == 2, inflow_state[None, None, :], distribution),
    )
    tables = twiddles(size_v)
    multipliers = jnp.concatenate(
        [
            gain_left.reshape(rank_count, size_v, plane_size),
            gain_right.reshape(rank_count, size_v, plane_size),
            loss_table.reshape(1, size_v, plane_size),
        ],
        0,
    )
    grouped = boundary_state.reshape(groups, -1, planes, plane_size)
    item_block = lax.all_to_all(grouped, "vert", split_axis=0, concat_axis=2, tiled=True)
    count = item_block.shape[1]
    cells = item_block.reshape(count, size_v, plane_size)
    collided = lax.map(
        lambda one_cell: collide_cell(one_cell, multipliers, rank_count, tables), cells
    )
    result = lax.all_to_all(
        collided.reshape(1, count, size_v, plane_size),
        "vert",
        split_axis=2,
        concat_axis=0,
        tiled=True,
    )
    collided_state = result.reshape(boundary_state.shape)
    padded = padded_2(collided_state, (("gx", 0), ("gy", 1)), 1)
    return transport(padded, upwind_side, lax.axis_index("vert") * planes, size_v)


def solution(mesh):
    placed = (
        P("gx", "gy", "vert"),
        P("gx", "gy"),
        P("vert"),
        P("vert"),
        P(None, "vert"),
        P(),
        P(),
        P(),
    )
    return jax.shard_map(
        on_device, mesh=mesh, in_specs=placed, out_specs=P("gx", "gy", "vert"), check_vma=False
    )
```

profile of v0, /device:TPU:1, one launch (start us, length us, event | category | flops | bytes accessed | tf_op | source)
XLA Modules:
  0.0 102.7 jit_solution(3554297745623114884)
XLA Ops:
  0.9 1.0 %select_select_fusion = f32[4,2,3456]{2,1,0:T(2,128)S(1)} fusion(f32[4,2,3456]{2,1,0:T(2,128)} %param.10, pred[4,2]{1,0:T(4,128)(4,1)S(1)} %copy.24, pred[4,2]{1,0:T(4,128)(4,1)S(1)} %copy.23, f32[3456]{0:T(1024)} %param.13, f32[3456]{0:T(1024)} %param.12), kind=kLoop, calls=%fused_computation.53 | loop fusion | flops 55296 | bytes 248848 | tf_op jit(solution)/shard_map/jit(_where)/select_n | solution.py:94
  2.8 4.8 %all-to-all-start = ((f32[4,2,6,576]{3,1,2,0:T(2,128)}), f32[4,2,6,576]{3,1,2,0:T(2,128)}, u32[]{:S(2)}, u32[]{:S(2)}) async-start(f32[4,2,6,576]{3,1,2,0:T(2,128)} %copy.25), calls=%async_computation | async-start | bytes 245760 | tf_op jit(solution)/shard_map/all_to_all | solution.py:109
  7.9 6.2 %fusion.26 = (f32[1,576,576]{2,1,0:T(8,128)S(1)}, f32[1,576,576]{2,1,0:T(8,128)S(1)}) fusion(s32[576]{0:T(1024)S(1)} %get-tuple-element.98, s32[576]{0:T(1024)S(1)} %get-tuple-element.99), kind=kLoop, calls=%fused_computation.38 | loop fusion | flops 3981312 | bytes 2658816 | tf_op jit(solution)/shard_map/cos | solution.py:44
  14.0 7.6 %fusion.27 = (f32[576,1,576]{2,0,1:T(8,128)}, f32[576,1,576]{2,0,1:T(8,128)}) fusion(s32[576]{0:T(1024)S(1)} %get-tuple-element.98, s32[576]{0:T(1024)S(1)} %get-tuple-element.99), kind=kLoop, calls=%fused_computation.39 | loop fusion | flops 3981312 | bytes 2658816 | tf_op jit(solution)/shard_map/cos | solution.py:44
  21.7 2.4 %reshape.567 = f32[4,24,576]{2,1,0:T(8,128)} reshape(f32[4,24,24,24]{3,2,1,0:T(8,128)} %param.15) | data formatting | bytes 442368 | tf_op jit(solution)/shard_map/reshape | solution.py:102
  24.0 2.3 %reshape.568 = f32[4,24,576]{2,1,0:T(8,128)} reshape(f32[4,24,24,24]{3,2,1,0:T(8,128)} %param.16) | data formatting | bytes 442368 | tf_op jit(solution)/shard_map/reshape | solution.py:103
  27.1 1.9 %maximum_multiply_fusion = f32[2,576,576]{2,1,0:T(8,128)} fusion(f32[1,576,576]{2,1,0:T(8,128)S(1)} %get-tuple-element.93, f32[1,576,576]{2,1,0:T(8,128)S(1)} %get-tuple-element.92), kind=kLoop, calls=%fused_computation.21 | loop fusion | flops 1327104 | bytes 5308416 | tf_op jit(solution)/shard_map/div | solution.py:47
  29.0 1.0 copy-done.2
  31.7 19.7 %while.10 = (s32[]{:T(128)}, f32[2,24,576]{2,0,1:T(2,128)}, f32[2,24,576]{2,0,1:T(2,128)}, f32[576,2,576]{2,0,1:T(8,128)S(1)}, f32[2,24,2,24]{3,1,2,0:T(8,128)S(...) while((s32[]{:T(128)}, f32[2,24,576]{2,0,1:T(2,128)}, ...), condition=%wide.region_2.3_spmd, body=%wide.region_0.2_spmd.sunk | while | flops 2070683136 | bytes 20514980 | solution.py:112
  32.7 1.6 %convolution_bitcast_fusion.6 = f32[2,24,576,1]{2,1,0,3:T(8,128)S(1)} fusion(f32[576,2,576]{2,0,1:T(8,128)S(1)} %get-tuple-element.176, f32[1,24,576]{2,0,1:T(1,128)S(1)} %constant_dynamic-slice_fusion.2), kind=kOutput, calls=%fused_computation.5.clone.1 | convolution fusion | flops 191102976 | bytes 2820096 | tf_op jit(solution)/shard_map/while/body/eval_jaxpr/xj,jpk->pxk/dot_general | solution.py:53
  34.6 1.1 %convolution_bitcast_fusion.8 = f32[9,2,24,576]{3,2,1,0:T(8,128)S(1)} fusion(f32[9,24,576]{2,1,0:T(8,128)S(1)} %get-tuple-element.178, f32[2,24,576]{2,1,0:T(8,128)S(1)} %convolution_bitcast_fusion.7, f32[2,24,2,24]{3,1,2,0:T(8,128)S(1)} %copy-done.3), kind=kOutput, calls=%fused_computation.2.clone.1 | convolution fusion | flops 143576064 | bytes 1612800 | tf_op jit(solution)/shard_map/while/body/eval_jaxpr/pkqj,tqjz->tpkz/dot_general | solution.py:56
  35.7 3.1 %fusion.97 = f32[9,24,576]{2,1,0:T(8,128)S(1)} fusion(f32[9,2,24,576]{3,2,1,0:T(8,128)S(1)} %convolution_bitcast_fusion.8, f32[2,576,576]{2,1,0:T(8,128)S(1)} %copy-done), kind=kOutput, calls=%fused_computation.3.clone.1 | convolution fusion | flops 1719926784 | bytes 4147200 | tf_op jit(solution)/shard_map/while/body/eval_jaxpr/tqxj,qjk->txk/dot_general | solution.py:57
  39.6 2.0 %dynamic_update_slice.5 = f32[2,24,576]{2,0,1:T(2,128)} dynamic-update-slice(f32[2,24,576]{2,0,1:T(2,128)} %get-tuple-element.164, f32[1,24,576]{2,0,1:T(1,128)} %copy.48, s32[]{:T(128)} %get-tuple-element.163, s32[]{:T(128)} %constant.82.clone.1..sunk, s32[]{:T(128)} %constant.82.clone.1..sunk) | dynamic-update-slice | bytes 110596 | tf_op jit(solution)/shard_map/while/body/jit(dynamic_update_index_in_dim)/dynamic_update_slice | solution.py:112
  42.6 1.6 %convolution_bitcast_fusion.6 = f32[2,24,576,1]{2,1,0,3:T(8,128)S(1)} fusion(f32[576,2,576]{2,0,1:T(8,128)S(1)} %get-tuple-element.176, f32[1,24,576]{2,0,1:T(1,128)S(1)} %constant_dynamic-slice_fusion.2), kind=kOutput, calls=%fused_computation.5.clone.1 | convolution fusion | flops 191102976 | bytes 2820096 | tf_op jit(solution)/shard_map/while/body/eval_jaxpr/xj,jpk->pxk/dot_general | solution.py:53
  44.4 1.1 %convolution_bitcast_fusion.8 = f32[9,2,24,576]{3,2,1,0:T(8,128)S(1)} fusion(f32[9,24,576]{2,1,0:T(8,128)S(1)} %get-tuple-element.178, f32[2,24,576]{2,1,0:T(8,128)S(1)} %convolution_bitcast_fusion.7, f32[2,24,2,24]{3,1,2,0:T(8,128)S(1)} %copy-done.3), kind=kOutput, calls=%fused_computation.2.clone.1 | convolution fusion | flops 143576064 | bytes 1612800 | tf_op jit(solution)/shard_map/while/body/eval_jaxpr/pkqj,tqjz->tpkz/dot_general | solution.py:56
  45.6 3.1 %fusion.97 = f32[9,24,576]{2,1,0:T(8,128)S(1)} fusion(f32[9,2,24,576]{3,2,1,0:T(8,128)S(1)} %convolution_bitcast_fusion.8, f32[2,576,576]{2,1,0:T(8,128)S(1)} %copy-done), kind=kOutput, calls=%fused_computation.3.clone.1 | convolution fusion | flops 1719926784 | bytes 4147200 | tf_op jit(solution)/shard_map/while/body/eval_jaxpr/tqxj,qjk->txk/dot_general | solution.py:57
  49.4 2.0 %dynamic_update_slice.5 = f32[2,24,576]{2,0,1:T(2,128)} dynamic-update-slice(f32[2,24,576]{2,0,1:T(2,128)} %get-tuple-element.164, f32[1,24,576]{2,0,1:T(1,128)} %copy.48, s32[]{:T(128)} %get-tuple-element.163, s32[]{:T(128)} %constant.82.clone.1..sunk, s32[]{:T(128)} %constant.82.clone.1..sunk) | dynamic-update-slice | bytes 110596 | tf_op jit(solution)/shard_map/while/body/jit(dynamic_update_index_in_dim)/dynamic_update_slice | solution.py:112
  51.4 9.0 %all_to_all.30 = f32[1,2,24,576]{3,1,0,2:T(2,128)S(1)} all-to-all(f32[1,2,24,576]{3,1,0,2:T(2,128)} %bitcast.91), channel_id=1, replica_groups=mesh['gx'=16,'gy'=8,'vert'=4] {'vert'}, dimensions={2} | all-to-all | bytes 221184 | tf_op jit(solution)/shard_map/all_to_all | solution.py:115
  60.5 18.0 %collective-permute-start = (f32[1,2,3456]{2,1,0:T(2,128)S(1)}, f32[1,2,3456]{2,1,0:T(2,128)S(1)}, u32[]{:S(2)}, u32[]{:S(2)}) collective-permute-start(f32[1,2,3456]{2,1,0:T(2,128)S(1)} %slice.51), channel_id=1, source_target_pairs={{0,32},{32,64},{64,96},{96,128},{128,160},{160,192},{192,224},{224... | collective-permute-start | bytes 82952 | tf_op jit(solution)/shard_map/ppermute | solution.py:18
  79.7 1.9 %collective-permute-start.1 = (f32[1,2,3456]{2,1,0:T(2,128)S(1)}, f32[1,2,3456]{2,1,0:T(2,128)S(1)}, u32[]{:S(2)}, u32[]{:S(2)}) collective-permute-start(f32[1,2,3456]{2,1,0:T(2,128)S(1)} %slice.54), channel_id=1, source_target_pairs={{32,0},{64,32},{96,64},{128,96},{160,128},{192,160},{224,192},{256... | collective-permute-start | bytes 82952 | tf_op jit(solution)/shard_map/ppermute | solution.py:19
  81.7 11.9 %collective-permute-done.1 = f32[1,2,3456]{2,1,0:T(2,128)S(1)} collective-permute-done((f32[1,2,3456]{2,1,0:T(2,128)S(1)}, f32[1,2,3456]{2,1,0:T(2,128)S(1)}, u32[]{:S(2)}, u32[]{:S(2)}) %collective-permute-start.1) | collective-permute-done | bytes 27680 | tf_op jit(solution)/shard_map/ppermute | solution.py:19
  93.8 2.8 %collective-permute-start.2 = (f32[6,1,3456]{2,1,0:T(1,128)S(1)}, f32[6,1,3456]{2,1,0:T(1,128)S(1)}, u32[]{:S(2)}, u32[]{:S(2)}) collective-permute-start(f32[6,1,3456]{2,1,0:T(1,128)S(1)} %get-tuple-element.82), channel_id=1, source_target_pairs={{0,4},{4,8},{8,12},{12,16},{16,20},{20,24},{24,28},{1,5},{5,9},{9,... | collective-permute-start | bytes 248840 | tf_op jit(solution)/shard_map/ppermute | solution.py:18
  96.6 1.3 %collective-permute-start.3 = (f32[6,1,3456]{2,1,0:T(1,128)S(1)}, f32[6,1,3456]{2,1,0:T(1,128)S(1)}, u32[]{:S(2)}, u32[]{:S(2)}) collective-permute-start(f32[6,1,3456]{2,1,0:T(1,128)S(1)} %get-tuple-element.83), channel_id=1, source_target_pairs={{4,0},{8,4},{12,8},{16,12},{20,16},{24,20},{28,24},{5,1},{9,5},{13... | collective-permute-start | bytes 248840 | tf_op jit(solution)/shard_map/ppermute | solution.py:19
  98.0 3.7 %collective-permute-done.3 = f32[6,1,3456]{2,1,0:T(1,128)S(1)} collective-permute-done((f32[6,1,3456]{2,1,0:T(1,128)S(1)}, f32[6,1,3456]{2,1,0:T(1,128)S(1)}, u32[]{:S(2)}, u32[]{:S(2)}) %collective-permute-start.3) | collective-permute-done | bytes 82976 | tf_op jit(solution)/shard_map/ppermute | solution.py:19
  (61 shorter events, 11.1 us)
Async XLA Ops:
  2.8 28.9 %all-to-all-start = ((f32[4,2,6,576]{3,1,2,0:T(2,128)}), f32[4,2,6,576]{3,1,2,0:T(2,128)}, u32[]{:S(2)}, u32[]{:S(2)}) async-start(f32[4,2,6,576]{3,1,2,0:T(2,128)} %copy.25), calls=%async_computation | async-start | bytes 245760 | tf_op jit(solution)/shard_map/all_to_all | solution.py:109
  21.7 4.7 %copy-start.6 = (f32[24,24,24]{2,1,0:T(8,128)S(1)}, f32[24,24,24]{2,1,0:T(8,128)}, u32[]{:S(2)}) copy-start(f32[24,24,24]{2,1,0:T(8,128)} %param.17) | copy-start | bytes 165892
  27.1 1.9 %copy-start.1 = (f32[576,1,576]{2,0,1:T(8,128)S(1)}, f32[576,1,576]{2,0,1:T(8,128)}, u32[]{:S(2)}) copy-start(f32[576,1,576]{2,0,1:T(8,128)} %get-tuple-element.94) | copy-start | bytes 3981316
  27.1 2.9 %copy-start.2 = (f32[576,1,576]{2,0,1:T(8,128)S(1)}, f32[576,1,576]{2,0,1:T(8,128)}, u32[]{:S(2)}) copy-start(f32[576,1,576]{2,0,1:T(8,128)} %get-tuple-element.95) | copy-start | bytes 3981316
  30.0 0.9 copy-start.4
  30.0 1.1 %copy-start.5 = (f32[4,24,576]{2,1,0:T(8,128)S(1)}, f32[4,24,576]{2,1,0:T(8,128)}, u32[]{:S(2)}) copy-start(f32[4,24,576]{2,1,0:T(8,128)} %reshape.568) | copy-start | bytes 663556
  30.0 1.1 %copy-start.7 = (f32[1,24,576]{2,1,0:T(8,128)S(1)}, f32[1,24,576]{2,1,0:T(8,128)}, u32[]{:S(2)}) copy-start(f32[1,24,576]{2,1,0:T(8,128)} %reshape.569) | copy-start | bytes 165892
  32.7 1.9 %copy-start.3 = (f32[2,24,2,24]{3,1,2,0:T(8,128)S(1)}, f32[2,24,2,24]{3,1,2,0:T(8,128)}, u32[]{:S(2)}) copy-start(f32[2,24,2,24]{3,1,2,0:T(8,128)} %get-tuple-element.179) | copy-start | bytes 27652 | tf_op jit(solution)/shard_map/while
  32.7 3.0 %copy-start = (f32[2,576,576]{2,1,0:T(8,128)S(1)}, f32[2,576,576]{2,1,0:T(8,128)}, u32[]{:S(2)}) copy-start(f32[2,576,576]{2,1,0:T(8,128)} %get-tuple-element.180) | copy-start | bytes 7962628 | tf_op jit(solution)/shard_map/while
  42.5 1.9 %copy-start.3 = (f32[2,24,2,24]{3,1,2,0:T(8,128)S(1)}, f32[2,24,2,24]{3,1,2,0:T(8,128)}, u32[]{:S(2)}) copy-start(f32[2,24,2,24]{3,1,2,0:T(8,128)} %get-tuple-element.179) | copy-start | bytes 27652 | tf_op jit(solution)/shard_map/while
  42.5 3.0 %copy-start = (f32[2,576,576]{2,1,0:T(8,128)S(1)}, f32[2,576,576]{2,1,0:T(8,128)}, u32[]{:S(2)}) copy-start(f32[2,576,576]{2,1,0:T(8,128)} %get-tuple-element.180) | copy-start | bytes 7962628 | tf_op jit(solution)/shard_map/while
  60.5 21.1 %collective-permute-start = (f32[1,2,3456]{2,1,0:T(2,128)S(1)}, f32[1,2,3456]{2,1,0:T(2,128)S(1)}, u32[]{:S(2)}, u32[]{:S(2)}) collective-permute-start(f32[1,2,3456]{2,1,0:T(2,128)S(1)} %slice.51), channel_id=1, source_target_pairs={{0,32},{32,64},{64,96},{96,128},{128,160},{160,192},{192,224},{224... | collective-permute-start | bytes 82952 | tf_op jit(solution)/shard_map/ppermute | solution.py:18
  79.7 13.9 %collective-permute-start.1 = (f32[1,2,3456]{2,1,0:T(2,128)S(1)}, f32[1,2,3456]{2,1,0:T(2,128)S(1)}, u32[]{:S(2)}, u32[]{:S(2)}) collective-permute-start(f32[1,2,3456]{2,1,0:T(2,128)S(1)} %slice.54), channel_id=1, source_target_pairs={{32,0},{64,32},{96,64},{128,96},{160,128},{192,160},{224,192},{256... | collective-permute-start | bytes 82952 | tf_op jit(solution)/shard_map/ppermute | solution.py:19
  93.8 4.3 %collective-permute-start.2 = (f32[6,1,3456]{2,1,0:T(1,128)S(1)}, f32[6,1,3456]{2,1,0:T(1,128)S(1)}, u32[]{:S(2)}, u32[]{:S(2)}) collective-permute-start(f32[6,1,3456]{2,1,0:T(1,128)S(1)} %get-tuple-element.82), channel_id=1, source_target_pairs={{0,4},{4,8},{8,12},{12,16},{16,20},{20,24},{24,28},{1,5},{5,9},{9,... | collective-permute-start | bytes 248840 | tf_op jit(solution)/shard_map/ppermute | solution.py:18
  96.6 5.2 %collective-permute-start.3 = (f32[6,1,3456]{2,1,0:T(1,128)S(1)}, f32[6,1,3456]{2,1,0:T(1,128)S(1)}, u32[]{:S(2)}, u32[]{:S(2)}) collective-permute-start(f32[6,1,3456]{2,1,0:T(1,128)S(1)} %get-tuple-element.83), channel_id=1, source_target_pairs={{4,0},{8,4},{12,8},{16,12},{20,16},{24,20},{28,24},{5,1},{9,5},{13... | collective-permute-start | bytes 248840 | tf_op jit(solution)/shard_map/ppermute | solution.py:19
where the time goes:
time: 103 us
  starting transfers between devices  28.8 us (28%)
  other arithmetic  20.5 us (20%)
  local copies, waits for them, and re-layouts  16.2 us (16%)
  waiting for transfers between devices  15.8 us (15%)
  matrix products  12.1 us (12%)
  blocking collectives  9.02 us (9%)
    ppermute x2, starting transfers between devices, padded_2(): before = lax.ppermute(last, axis, up)  20.8 us
    ppermute x2, waiting for transfers between devices, padded_2(): after = lax.ppermute(leading, axis, down)  15.6 us
    cos x2, other arithmetic, twiddles(): plane_cos = jnp.cos(plane_phases)  13.8 us
    all_to_all x1, blocking collectives, on_device(): lax.all_to_all(collided.reshape(1, count, size_v, plane_size), 'vert', sp...  9.02 us
    dot_general x2, matrix products, collide_cell(): jnp.einsum('tqxj,qjk->txk', shaped, plane_inverse, precision=highest)  6.16 us
    dynamic_update_slice x4, local copies, waits for them, and re-layouts, on_device(): lax.map(lambda one_cell: collide_cell(one_cell, multipliers, rank_count,...  5.38 us
    all_to_all x1, starting transfers between devices, on_device(): lax.all_to_all(grouped, 'vert', split_axis=0, concat_axis=2, tiled=True)  4.84 us
    ppermute x2, starting transfers between devices, padded_2(): after = lax.ppermute(leading, axis, down)  3.21 us
  transfers between devices with their start and end apart: 5, of which 3 were waited for; matrix products, arithmetic and copies ran while one was open for 23% of the time, Pallas kernels for 0%

commit v1 on v0

v1 whole, which is shorter than its diff:
```python
import functools

import jax
import jax.numpy as jnp
import ml_dtypes
import numpy as np
from jax import lax
from jax.experimental import pallas as pl
from jax.experimental.pallas import tpu as pltpu
from jax.sharding import PartitionSpec as P

MESH = pl.DeviceIdType.MESH
F32 = jnp.float32
BF16 = jnp.bfloat16

V = 24
PLANE = V * V
HALF = V // 2
RANK = 4
TABLES = 2 * RANK + 1
GROUPS = 4
NX, NY = 4, 2
SLAB = PLANE * V // GROUPS
LANES = 128
ROWS = SLAB // LANES
BLOCK = 56
EDGE = 32
PAIRS = 3
CHUNKS = 2 * PLANE // LANES
W = 256
PACK = 5
GROUPED = 5 * LANES
SIGNS = ((1, 1), (1, -1), (-1, 1), (-1, -1))
COLLISION_STEP = 0.25
COURANT = 0.45


def split_constant(a):
    hi = a.astype(ml_dtypes.bfloat16)
    lo = (a - hi.astype(np.float64)).astype(ml_dtypes.bfloat16)
    return hi, lo


def chunked(a):
    pad = -a.shape[-1] % LANES
    a = np.pad(a, [(0, 0)] * (a.ndim - 1) + [(0, pad)])
    a = a.reshape(*a.shape[:-1], -1, LANES)
    return np.ascontiguousarray(np.moveaxis(a, -2, -3))


def stacked(a):
    hi, lo = split_constant(a)
    return chunked(np.concatenate([hi, hi, lo], axis=1))


@functools.cache
def constants():
    step = 2.0 * np.pi / V
    inner = [(a, b) for a in range(1, HALF) for b in range(1, HALF)]
    outer = [(a, b) for a in range(HALF + 1) for b in range(HALF + 1) if a % HALF == 0 or b % HALF == 0]
    points = np.array(inner + outer)
    count = len(points)
    qy, qz = points[:, 0], points[:, 1]
    natural = np.arange(PLANE)
    ny, nz = natural // V, natural % V
    trig = (np.cos, np.sin)
    classes = ((0, 0), (0, 1), (1, 0), (1, 1))

    def grid(rows_y, rows_z, cy, cz):
        by = trig[cy](step * (rows_y[:, None] * qy[None, :] % V))
        bz = trig[cz](step * (rows_z[:, None] * qz[None, :] % V))
        return by * bz

    plane_forward = np.zeros((PLANE, 4 * W))
    plane_inverse = np.zeros((4, W, W))
    weight = np.where(qy % HALF == 0, 0.5, 1.0) * np.where(qz % HALF == 0, 0.5, 1.0) / PLANE
    for c, (cy, cz) in enumerate(classes):
        plane_forward[:, c * W : c * W + count] = grid(ny, nz, cy, cz)
        plane_inverse[c, :count, :count] = weight[:, None] * grid(qy, qz, cy, cz)

    place = np.zeros((GROUPED, 4 * W))
    unplace = np.zeros((4 * W, PLANE))
    seen = set()
    for s, (sy, sz) in enumerate(SIGNS):
        for q in range(count):
            y, z = sy * qy[q] % V, sz * qz[q] % V
            place[(y // PACK) * LANES + (y % PACK) * V + z, s * W + q] = 1.0
            if (y, z) not in seen:
                seen.add((y, z))
                unplace[s * W + q, y * V + z] = 1.0

    row_of = np.zeros((2, V), dtype=int)
    for jx in range(V):
        pair, odd = jx // 2, jx % 2
        u, q = pair // PAIRS, pair % PAIRS
        for cell in range(2):
            row_of[cell, jx] = odd * V + 2 * PAIRS * u + PAIRS * cell + q
    k = np.arange(V)
    theta = step * (k[:, None] * k[None, :] % V)
    cos, sin = np.cos(theta), np.sin(theta)
    x_forward = np.zeros((2 * V, 2 * V))
    x_forward[:V, row_of[0]] = cos
    x_forward[:V, row_of[1]] = sin
    x_forward[V:, row_of[0]] = -sin
    x_forward[V:, row_of[1]] = cos
    real = np.concatenate([cos, -sin], axis=1)
    imag = np.concatenate([sin, cos], axis=1)
    x_inverse = []
    for first, second in ((real, imag), (-imag, real), (-imag, real), (-real, -imag)):
        m = np.zeros((2 * V, 2 * V))
        m[row_of[0]] = first
        m[row_of[1]] = second
        x_inverse.append(stacked(m / (2 * V)))

    reverse = np.zeros((32, 2 * V))
    for r in range(V):
        reverse[r, (V - r) % V] = 1.0
        reverse[r, V + (V - r) % V] = 1.0

    velocity = np.arange(PLANE * V)
    courant_x = COURANT * np.abs(2 * (velocity // PLANE) - (V - 1)).astype(np.float32) / (V - 1)
    courant_y = COURANT * np.abs(2 * (velocity // V % V) - (V - 1)).astype(np.float32) / (V - 1)
    courants = np.zeros((GROUPS, 2, EDGE, LANES), np.float32)
    courants[:, 0, :ROWS] = courant_x.reshape(GROUPS, ROWS, LANES)
    courants[:, 1, :ROWS] = courant_y.reshape(GROUPS, ROWS, LANES)

    return {
        "x_forward": stacked(x_forward),
        "x_inverse": np.stack(x_inverse),
        "plane_forward": chunked(np.stack(split_constant(plane_forward))),
        "plane_inverse": chunked(np.stack(split_constant(plane_inverse))),
        "place": chunked(place.astype(ml_dtypes.bfloat16)),
        "unplace": chunked(unplace.astype(ml_dtypes.bfloat16)),
        "reverse": reverse.astype(ml_dtypes.bfloat16),
        "courants": courants,
    }


NAMES = ("x_forward", "x_inverse", "plane_forward", "plane_inverse", "place", "unplace", "reverse", "courants")


def halves(a):
    hi = a.astype(BF16)
    lo = (a - hi.astype(F32)).astype(BF16)
    return hi, lo


def wide(ref, start, count, width=None):
    a = jnp.concatenate([ref[start + i] for i in range(count)], axis=1)
    return a if width is None else a[:, :width]


def dot(a, b):
    return jnp.dot(a, b, preferred_element_type=F32)


def quadrants(a, b, c, d):
    p, m = a + b, a - b
    q, r = c + d, c - d
    return p + q, m + r, p - q, m - r


def kernel(
    sizes,
    dist_hbm, kinds_ref, wall_hbm, inflow_hbm, side_hbm, left_hbm, right_hbm, loss_hbm,
    xf_hbm, xi_hbm, pf_hbm, pi_hbm, place_hbm, unplace_hbm, reverse_hbm, courants_hbm,
    out_ref,
    dist, dense, wall, inflow, side, raw, xf, xi, pf, pi, place, unplace, reverse, courants,
    sides, packed, quads, table, send, recv, field, shaped_hi, shaped_lo, planes, collided, back, own, from_y, from_x,
    local_sem, send1, recv1, send_own, recv_own, send_y, recv_y, send_x, recv_x,
):
    n_gx, n_gy = sizes
    gx, gy, me = lax.axis_index("gx"), lax.axis_index("gy"), lax.axis_index("vert")
    my_y, my_h = lax.rem(me, 2), me // 2
    step_y, step_x = 2 * my_y - 1, 2 * my_h - 1
    to_y, to_x = gy + step_y, gx + step_x
    has_y = jnp.logical_and(to_y >= 0, to_y < n_gy)
    has_x = jnp.logical_and(to_x >= 0, to_x < n_gx)

    at_gain = RANK * V * PLANE // V
    pulls = [
        (dist_hbm, dist), (wall_hbm, wall), (inflow_hbm, inflow),
        (left_hbm, raw.at[pl.ds(0, at_gain)]), (right_hbm, raw.at[pl.ds(at_gain, at_gain)]),
        (loss_hbm, raw.at[pl.ds(2 * at_gain, PLANE)]), (place_hbm, place), (reverse_hbm, reverse),
        (xf_hbm, xf), (pf_hbm, pf), (xi_hbm, xi), (pi_hbm, pi), (unplace_hbm, unplace), (side_hbm, side),
        (courants_hbm.at[me], courants),
    ]
    pulls = [pltpu.make_async_copy(a, b, local_sem.at[i]) for i, (a, b) in enumerate(pulls)]
    for pull in pulls:
        pull.start()

    for edge, buffers in ((0, from_x), (n_gx - 1, from_x)):
        @pl.when(gx == edge)
        def _(edge=edge):
            from_x[0 if edge == 0 else 1] = jnp.zeros((2, EDGE, LANES), F32)

    for edge in (0, n_gy - 1):
        @pl.when(gy == edge)
        def _(edge=edge):
            from_y[0 if edge == 0 else 1] = jnp.zeros((2, BLOCK, LANES), F32)

    barrier = pltpu.get_barrier_semaphore()

    def greet(x, y, v):
        pl.semaphore_signal(barrier, inc=1, device_id=(x, y, v), device_id_type=MESH)

    for d in range(1, GROUPS):
        greet(gx, gy, lax.rem(me + d, GROUPS))
    for step in (-1, 1):
        @pl.when(jnp.logical_and(gy + step >= 0, gy + step < n_gy))
        def _(step=step):
            for h in range(2):
                greet(gx, gy + step, 2 * h + (1 if step < 0 else 0))

        @pl.when(jnp.logical_and(gx + step >= 0, gx + step < n_gx))
        def _(step=step):
            for y in range(2):
                greet(gx + step, gy, y + (2 if step < 0 else 0))

    for i in range(3):
        pulls[i].wait()
    for x in range(NX):
        for r in range(ROWS):
            at = (x * ROWS + r) * NY
            dense[at : at + NY, :] = dist[x, :, r * LANES : (r + 1) * LANES]
    for v in range(GROUPS):
        y, h = v % 2, v // 2
        send[v, pl.ds(48, 8)] = jnp.zeros((8, LANES), F32)
        for cell in range(2):
            x = 3 * h + (1 - 2 * h) * cell
            kind = jnp.full((ROWS, LANES), kinds_ref[y, x], jnp.int32)
            own_state = dense[pl.ds(x * 2 * ROWS + y, ROWS, stride=2), :]
            state = jnp.where(kind == 1, wall[...], jnp.where(kind == 2, inflow[...], own_state))
            send[v, pl.ds(cell * ROWS, ROWS)] = state
    recv[me] = send[me]

    pl.semaphore_wait(
        barrier, GROUPS - 1 + GROUPS * has_y.astype(jnp.int32) + GROUPS * has_x.astype(jnp.int32)
    )
    first = []
    for d in range(1, GROUPS):
        to = lax.rem(me + d, GROUPS)
        first.append(
            pltpu.make_async_remote_copy(
                src_ref=send.at[to], dst_ref=recv.at[me], send_sem=send1.at[d], recv_sem=recv1.at[d],
                device_id=(gx, gy, to), device_id_type=MESH,
            )
        )
        first[-1].start()

    for i in range(3, 8):
        pulls[i].wait()
    packed[...] = jnp.zeros_like(packed)
    for ky in range(V):
        at = (ky // PACK) * LANES + (ky % PACK) * V
        packed[:, at : at + V] = raw[pl.ds(ky, TABLES * V, stride=V), :]
    hi, lo = halves(packed[...])
    both = jnp.concatenate([hi, lo], axis=0)
    for s in range(4):
        q = dot(both, wide(place, 2 * s, 2))
        quads[s] = q[: TABLES * V] + q[TABLES * V :]

    def symmetrise(t, _):
        at = pl.ds(pl.multiple_of(t * V, 8), V)
        for s in range(4):
            hi, lo = halves(quads[3 - s, at])
            mirrored = dot(reverse[...], jnp.concatenate([hi, lo], axis=0))[:V]
            table[s, at] = quads[s, at] + mirrored
        return 0

    lax.fori_loop(0, TABLES, symmetrise, 0)

    pulls[13].wait()
    for r in range(ROWS):
        for k in range(2):
            sides[k, r : r + 1, :] = side[k : k + 1, r * LANES : (r + 1) * LANES]

    for i in range(8, 13):
        pulls[i].wait()
    for d in range(1, GROUPS):
        first[d - 1].wait_recv()
    for u in range(GROUPS):
        for c in range(CHUNKS):
            field[6 * u : 6 * u + 6, c * LANES : (c + 1) * LANES] = recv[u, pl.ds(c, 6, stride=CHUNKS), :]
    cells = jnp.concatenate([field[:, :PLANE], field[:, PLANE:]], axis=0)
    hi, lo = halves(cells)
    along_x = dot(wide(xf, 0, 2, 6 * V), jnp.concatenate([hi, lo, hi], axis=0))
    hi, lo = halves(along_x)
    both = jnp.concatenate([hi, lo], axis=0)
    parts = []
    for c in range(4):
        top = dot(both, wide(pf.at[0], 2 * c, 2))
        parts.append(top[: 2 * V] + top[2 * V :] + dot(hi, wide(pf.at[1], 2 * c, 2)))
    cc, cs, sc, ss = parts
    cos_cos, sin_sin = cc, -ss
    swapped = lambda a: jnp.concatenate([a[V:], -a[:V]], axis=0)
    spectrum = quadrants(cos_cos, swapped(cs), swapped(sc), sin_sin)

    for t in range(TABLES):
        at = slice(t * V, (t + 1) * V)
        a = []
        for s in range(4):
            m = table[s, at]
            a.append(jnp.concatenate([spectrum[s][:V] * m, spectrum[s][V:] * m], axis=0))
        for c, b in enumerate(quadrants_to_classes(*a)):
            hi, lo = halves(b)
            z = dot(wide(xi.at[c], 0, 2, 6 * V), jnp.concatenate([hi, lo, hi], axis=0))
            hi, lo = halves(z)
            shaped_hi[c, t * 2 * V : (t + 1) * 2 * V] = hi
            shaped_lo[c, t * 2 * V : (t + 1) * 2 * V] = lo
    for c in range(4):
        top, low = wide(pi.at[0, c], 0, 2), wide(pi.at[1, c], 0, 2)
        planes[c] = dot(shaped_hi[c], top) + dot(shaped_lo[c], top) + dot(shaped_hi[c], low)

    def fields(t):
        at = slice(t * 2 * V, (t + 1) * 2 * V)
        return quadrants(*(planes[c, at] for c in range(4)))

    gain = [0.0] * 4
    for r in range(RANK):
        gain = [g + a * b for g, a, b in zip(gain, fields(r), fields(RANK + r))]
    rates = jnp.concatenate(
        [jnp.concatenate(list(gain), axis=1), jnp.concatenate(list(fields(2 * RANK)), axis=1)], axis=0
    )
    hi, lo = halves(rates)
    rates = dot(jnp.concatenate([hi, lo], axis=0), wide(unplace, 0, 5, PLANE))
    rates = rates[: 4 * V] + rates[4 * V :]
    result = cells + COLLISION_STEP * (rates[: 2 * V] - cells * rates[2 * V :])
    collided[:, :PLANE] = result[:V]
    collided[:, PLANE:] = result[V:]
    for u in range(GROUPS):
        back[u, pl.ds(48, 8)] = jnp.zeros((8, LANES), F32)
        for c in range(CHUNKS):
            back[u, pl.ds(c, 6, stride=CHUNKS), :] = collided[6 * u : 6 * u + 6, c * LANES : (c + 1) * LANES]

    def push_x(u):
        return pltpu.make_async_remote_copy(
            src_ref=back.at[u, pl.ds(0, EDGE)], dst_ref=from_x.at[1 - my_h, my_y],
            send_sem=send_x.at[u], recv_sem=recv_x.at[1 - my_h, my_y],
            device_id=(to_x, gy, u), device_id_type=MESH,
        )

    def push_y(u):
        return pltpu.make_async_remote_copy(
            src_ref=back.at[u], dst_ref=from_y.at[1 - my_y, my_h],
            send_sem=send_y.at[u], recv_sem=recv_y.at[1 - my_y, my_h],
            device_id=(gx, to_y, u), device_id_type=MESH,
        )

    def push_own(d):
        to = lax.rem(me + d, GROUPS)
        return pltpu.make_async_remote_copy(
            src_ref=back.at[to], dst_ref=own.at[me], send_sem=send_own.at[d], recv_sem=recv_own.at[d],
            device_id=(gx, gy, to), device_id_type=MESH,
        )

    @pl.when(has_x)
    def _():
        for u in range(GROUPS):
            push_x(u).start()

    @pl.when(has_y)
    def _():
        for u in range(GROUPS):
            push_y(u).start()

    for d in range(1, GROUPS):
        push_own(d).start()
    own[me] = back[me]

    pulls[14].wait()
    for d in range(1, GROUPS):
        push_own(d).wait_recv()
    for step in (-1, 1):
        k = 0 if step < 0 else 1

        @pl.when(jnp.logical_and(gy + step >= 0, gy + step < n_gy))
        def _(k=k):
            for h in range(2):
                pltpu.make_async_remote_copy(
                    src_ref=back.at[0], dst_ref=from_y.at[k, h], send_sem=send_y.at[0], recv_sem=recv_y.at[k, h],
                    device_id=(gx, to_y, me), device_id_type=MESH,
                ).wait_recv()

        @pl.when(jnp.logical_and(gx + step >= 0, gx + step < n_gx))
        def _(k=k):
            for y in range(2):
                pltpu.make_async_remote_copy(
                    src_ref=back.at[0, pl.ds(0, EDGE)], dst_ref=from_x.at[k, y], send_sem=send_x.at[0],
                    recv_sem=recv_x.at[k, y], device_id=(to_x, gy, me), device_id_type=MESH,
                ).wait_recv()

    def at_cell(ref, x):
        cell = (0, 1, 1, 0)[x]
        return ref[pl.ds(cell * ROWS, ROWS), :]

    courant_x, courant_y = courants[0, pl.ds(0, ROWS)], courants[1, pl.ds(0, ROWS)]
    higher_x, higher_y = sides[0] == 1, sides[1] == 1
    centre = {(x, y): at_cell(own.at[y + 2 * (x // 2)], x) for x in range(NX) for y in range(NY)}
    for x in range(NX):
        for y in range(NY):
            here = centre[x, y]
            below_x = centre[x - 1, y] if x > 0 else from_x[0, y, pl.ds(0, ROWS)]
            above_x = centre[x + 1, y] if x < NX - 1 else from_x[1, y, pl.ds(0, ROWS)]
            below_y = centre[x, 0] if y > 0 else at_cell(from_y.at[0, x // 2], x)
            above_y = centre[x, 1] if y < 1 else at_cell(from_y.at[1, x // 2], x)
            up_x = jnp.where(higher_x, below_x, above_x)
            up_y = jnp.where(higher_y, below_y, above_y)
            dense[pl.ds(x * 2 * ROWS + y, ROWS, stride=2), :] = (
                here - courant_x * (here - up_x) - courant_y * (here - up_y)
            )
        for r in range(ROWS):
            at = (x * ROWS + r) * NY
            out_ref[x, :, r * LANES : (r + 1) * LANES] = dense[at : at + NY, :]

    for d in range(1, GROUPS):
        first[d - 1].wait_send()
        push_own(d).wait_send()

    @pl.when(has_y)
    def _():
        for u in range(GROUPS):
            push_y(u).wait_send()

    @pl.when(has_x)
    def _():
        for u in range(GROUPS):
            push_x(u).wait_send()


def quadrants_to_classes(pp, pm, mp, mm):
    a, b = pp + pm, pp - pm
    c, d = mp + mm, mp - mm
    return a + c, b + d, a - c, b - d


def on_device(sizes, distribution, cell_types, wall_state, inflow_state, upwind_side, gain_left, gain_right, loss_table):
    tables = constants()
    tables = [jnp.asarray(tables[name]) for name in NAMES]
    operands = [
        distribution,
        cell_types.T,
        wall_state.reshape(ROWS, LANES),
        inflow_state.reshape(ROWS, LANES),
        upwind_side,
        gain_left.reshape(RANK * PLANE, V),
        gain_right.reshape(RANK * PLANE, V),
        loss_table.reshape(PLANE, V),
        *tables,
    ]
    spaces = [pl.BlockSpec(memory_space=pl.ANY)] * len(operands)
    spaces[1] = pl.BlockSpec(memory_space=pltpu.SMEM)
    dma = pltpu.SemaphoreType.DMA
    held = [
        pltpu.VMEM((NX, NY, SLAB), F32),
        pltpu.VMEM((NX * NY * ROWS, LANES), F32),
        pltpu.VMEM((ROWS, LANES), F32),
        pltpu.VMEM((ROWS, LANES), F32),
        pltpu.VMEM((2, SLAB), jnp.int32),
        pltpu.VMEM((TABLES * PLANE, V), F32),
        *(pltpu.VMEM(t.shape, t.dtype) for t in tables[:-1]),
        pltpu.VMEM(tables[-1].shape[1:], F32),
        pltpu.VMEM((2, ROWS, LANES), jnp.int32),
        pltpu.VMEM((TABLES * V, GROUPED), F32),
        pltpu.VMEM((4, TABLES * V, W), F32),
        pltpu.VMEM((4, TABLES * V, W), F32),
        pltpu.VMEM((GROUPS, BLOCK, LANES), F32),
        pltpu.VMEM((GROUPS, BLOCK, LANES), F32),
        pltpu.VMEM((V, 2 * PLANE), F32),
        pltpu.VMEM((4, TABLES * 2 * V, W), BF16),
        pltpu.VMEM((4, TABLES * 2 * V, W), BF16),
        pltpu.VMEM((4, TABLES * 2 * V, W), F32),
        pltpu.VMEM((V, 2 * PLANE), F32),
        pltpu.VMEM((GROUPS, BLOCK, LANES), F32),
        pltpu.VMEM((GROUPS, BLOCK, LANES), F32),
        pltpu.VMEM((2, 2, BLOCK, LANES), F32),
        pltpu.VMEM((2, 2, EDGE, LANES), F32),
        dma((15,)),
        dma((GROUPS,)), dma((GROUPS,)),
        dma((GROUPS,)), dma((GROUPS,)),
        dma((GROUPS,)), dma((2, 2)),
        dma((GROUPS,)), dma((2, 2)),
    ]
    return pl.pallas_call(
        functools.partial(kernel, sizes),
        out_shape=jax.ShapeDtypeStruct((NX, NY, SLAB), F32),
        in_specs=spaces,
        out_specs=pl.BlockSpec(memory_space=pltpu.VMEM),
        scratch_shapes=held,
        compiler_params=pltpu.CompilerParams(
            collective_id=0, has_side_effects=True, vmem_limit_bytes=60 * 1024 * 1024
        ),
        cost_estimate=pl.CostEstimate(flops=3_000_000_000, bytes_accessed=10_000_000, transcendentals=0),
        name="step",
    )(*operands)


def solution(mesh):
    placed = (
        P("gx", "gy", "vert"),
        P("gx", "gy"),
        P("vert"),
        P("vert"),
        P(None, "vert"),
        P(),
        P(),
        P(),
    )
    sizes = (mesh.shape["gx"], mesh.shape["gy"])
    return jax.shard_map(
        functools.partial(on_device, sizes),
        mesh=mesh,
        in_specs=placed,
        out_specs=P("gx", "gy", "vert"),
        check_vma=False,
    )
```

time: 103 us -> 32.9 us (0.32)
  the two profiles are of different devices: /device:TPU:1 before, /device:TPU:8 now
where the time goes in v1:
time: 32.9 us; the launch traced here: 32.8 us
  Pallas kernels  31.2 us (95%)
  local copies, waits for them, and re-layouts  1.55 us (5%)
    pallas_call x1, Pallas kernels, on_device(): pl.pallas_call(functools.partial(kernel, sizes), out_shape=jax.ShapeDtype...  31.2 us
    unnamed x1, local copies, waits for them, and re-layouts  1.55 us

profile of v1, /device:TPU:8, one launch (start us, length us, event | category | flops | bytes accessed | tf_op | source)
XLA Modules:
  0.0 32.8 jit_solution(11498808474765461931)
XLA Ops:
  0.0 31.2 %step.1 = f32[4,2,3456]{2,1,0:T(2,128)} custom-call(f32[4,2,3456]{2,1,0:T(2,128)} %dist_hbm.1, s32[2,4]{1,0:T(2,128)} %bitcast.11, f32[27,128]{1,0:T(8,128)} %bitcast.9, f32[27,128]{1,0:T(8,128)} %bitcast.10, s32[2,3456]{1,0:T(2,128)} %side_hbm.1, f32[2304,24]{1,0:T(8,128)} %bitcast.6, f32[2304,24]{1,0:T(8,128)} %bitcast.7, f32[576,24]{1,0:T(8,128)} %bitcast.8, ...), custom_call_target="tpu_custom_call" | custom-call | flops 3000000000 | bytes 10000000 | tf_op jit(solution)/shard_map/step/pallas_call | solution.py:484
  31.2 1.6 %copy.18 = f32[4,2,3456]{2,1,0:T(2,128)} copy(f32[4,2,3456]{2,1,0:T(2,128)} %step.1) | data formatting | bytes 221184

commit v2 on v1

--- a/solution.py
+++ b/solution.py
@@ -167,7 +167,7 @@
     out_ref,
     dist, dense, wall, inflow, side, raw, xf, xi, pf, pi, place, unplace, reverse, courants,
     sides, packed, quads, table, send, recv, field, shaped_hi, shaped_lo, planes, collided, back, own, from_y, from_x,
-    local_sem, send1, recv1, send_own, recv_own, send_y, recv_y, send_x, recv_x,
+    local_sem, send1, recv1, send_own, recv_own, send_y, recv_y, send_x, recv_x, ready,
 ):
     n_gx, n_gy = sizes
     gx, gy, me = lax.axis_index("gx"), lax.axis_index("gy"), lax.axis_index("vert")
@@ -176,6 +176,13 @@
     to_y, to_x = gy + step_y, gx + step_x
     has_y = jnp.logical_and(to_y >= 0, to_y < n_gy)
     has_x = jnp.logical_and(to_x >= 0, to_x < n_gx)
+    core = lax.rem(gx, 2)
+    early = lax.rem(gx // 2, 2) == 0
+    near_x, far_x = gx + 1 - 2 * core, gx - 1 + 2 * core
+    has_far = jnp.logical_and(far_x >= 0, far_x < n_gx)
+    sends_far = my_h == core
+    early_far = jnp.logical_and(has_far, early)
+    late_far = jnp.logical_and(has_far, jnp.logical_not(early))
 
     at_gain = RANK * V * PLANE // V
     pulls = [
@@ -189,15 +196,14 @@
     for pull in pulls:
         pull.start()
 
-    for edge, buffers in ((0, from_x), (n_gx - 1, from_x)):
-        @pl.when(gx == edge)
-        def _(edge=edge):
-            from_x[0 if edge == 0 else 1] = jnp.zeros((2, EDGE, LANES), F32)
-
-    for edge in (0, n_gy - 1):
-        @pl.when(gy == edge)
-        def _(edge=edge):
-            from_y[0 if edge == 0 else 1] = jnp.zeros((2, BLOCK, LANES), F32)
+    for k in range(2):
+        @pl.when(gx == k * (n_gx - 1))
+        def _(k=k):
+            from_x[k] = jnp.zeros((2, EDGE, LANES), F32)
+
+        @pl.when(gy == k * (n_gy - 1))
+        def _(k=k):
+            from_y[k] = jnp.zeros((2, BLOCK, LANES), F32)
 
     barrier = pltpu.get_barrier_semaphore()
 
@@ -212,10 +218,18 @@
             for h in range(2):
                 greet(gx, gy + step, 2 * h + (1 if step < 0 else 0))
 
-        @pl.when(jnp.logical_and(gx + step >= 0, gx + step < n_gx))
-        def _(step=step):
+    for y in range(2):
+        greet(near_x, gy, y + 2 * core)
+
+    @pl.when(early_far)
+    def _():
+        for y in range(2):
+            greet(far_x, gy, y + 2 * (1 - core))
+
+        @pl.when(sends_far)
+        def _():
             for y in range(2):
-                greet(gx + step, gy, y + (2 if step < 0 else 0))
+                greet(far_x, gy, y + 2 * core)
 
     for i in range(3):
         pulls[i].wait()
@@ -234,9 +248,8 @@
             send[v, pl.ds(cell * ROWS, ROWS)] = state
     recv[me] = send[me]
 
-    pl.semaphore_wait(
-        barrier, GROUPS - 1 + GROUPS * has_y.astype(jnp.int32) + GROUPS * has_x.astype(jnp.int32)
-    )
+    awaited = GROUPS - 1 + jnp.where(has_y, GROUPS, 0) + jnp.where(sends_far, 0, GROUPS)
+    pl.semaphore_wait(barrier, awaited + jnp.where(late_far, jnp.where(sends_far, GROUPS, 2), 0))
     first = []
     for d in range(1, GROUPS):
         to = lax.rem(me + d, GROUPS)
@@ -247,6 +260,13 @@
             )
         )
         first[-1].start()
+
+    @pl.when(late_far)
+    def _():
+        for y in range(2):
+            pl.semaphore_signal(
+                ready, inc=1, device_id=(far_x, gy, y + 2 * (1 - core)), device_id_type=MESH
+            )
 
     for i in range(3, 8):
         pulls[i].wait()
@@ -354,7 +374,7 @@
             device_id=(gx, gy, to), device_id_type=MESH,
         )
 
-    @pl.when(has_x)
+    @pl.when(jnp.logical_and(has_x, jnp.logical_not(jnp.logical_and(early, sends_far))))
     def _():
         for u in range(GROUPS):
             push_x(u).start()
@@ -367,6 +387,12 @@
     for d in range(1, GROUPS):
         push_own(d).start()
     own[me] = back[me]
+
+    @pl.when(jnp.logical_and(early_far, sends_far))
+    def _():
+        pl.semaphore_wait(ready, GROUPS)
+        for u in range(GROUPS):
+            push_x(u).start()
 
     pulls[14].wait()
     for d in range(1, GROUPS):
@@ -480,6 +506,7 @@
         dma((GROUPS,)), dma((GROUPS,)),
         dma((GROUPS,)), dma((2, 2)),
         dma((GROUPS,)), dma((2, 2)),
+        pltpu.SemaphoreType.REGULAR,
     ]
     return pl.pallas_call(
         functools.partial(kernel, sizes),

time: 32.9 us -> 30.3 us (0.921)
  the two profiles are of different devices: /device:TPU:8 before, /device:TPU:1 now
where the time goes in v2:
time: 30.3 us; the launch traced here: 30.2 us
  Pallas kernels  28.6 us (94%)
  local copies, waits for them, and re-layouts  1.55 us (5%)
    pallas_call x1, Pallas kernels, on_device(): pl.pallas_call(functools.partial(kernel, sizes), out_shape=jax.ShapeDtype...  28.6 us
    unnamed x1, local copies, waits for them, and re-layouts  1.55 us

profile of v2, /device:TPU:1, one launch (start us, length us, event | category | flops | bytes accessed | tf_op | source)
XLA Modules:
  0.0 30.2 jit_solution(8501135188848768292)
XLA Ops:
  0.0 28.6 %step.1 = f32[4,2,3456]{2,1,0:T(2,128)} custom-call(f32[4,2,3456]{2,1,0:T(2,128)} %dist_hbm.1, s32[2,4]{1,0:T(2,128)} %bitcast.11, f32[27,128]{1,0:T(8,128)} %bitcast.9, f32[27,128]{1,0:T(8,128)} %bitcast.10, s32[2,3456]{1,0:T(2,128)} %side_hbm.1, f32[2304,24]{1,0:T(8,128)} %bitcast.6, f32[2304,24]{1,0:T(8,128)} %bitcast.7, f32[576,24]{1,0:T(8,128)} %bitcast.8, ...), custom_call_target="tpu_custom_call" | custom-call | flops 3000000000 | bytes 10000000 | tf_op jit(solution)/shard_map/step/pallas_call | solution.py:511
  28.6 1.6 %copy.18 = f32[4,2,3456]{2,1,0:T(2,128)} copy(f32[4,2,3456]{2,1,0:T(2,128)} %step.1) | data formatting | bytes 221184

commit v3 on v2

--- a/solution.py
+++ b/solution.py
@@ -26,6 +26,7 @@
 BLOCK = 56
 EDGE = 32
 PAIRS = 3
+SOME = 16
 CHUNKS = 2 * PLANE // LANES
 W = 256
 PACK = 5
@@ -105,12 +106,17 @@
     x_forward[V:, row_of[1]] = cos
     real = np.concatenate([cos, -sin], axis=1)
     imag = np.concatenate([sin, cos], axis=1)
-    x_inverse = []
+    x_inverse, x_slab = [], [[] for _ in range(GROUPS)]
     for first, second in ((real, imag), (-imag, real), (-imag, real), (-real, -imag)):
         m = np.zeros((2 * V, 2 * V))
         m[row_of[0]] = first
         m[row_of[1]] = second
-        x_inverse.append(stacked(m / (2 * V)))
+        m = m / (2 * V)
+        x_inverse.append(stacked(m))
+        for u in range(GROUPS):
+            own = np.zeros((SOME, 2 * V))
+            own[:6], own[6:12] = m[6 * u : 6 * u + 6], m[V + 6 * u : V + 6 * u + 6]
+            x_slab[u].append(stacked(own))
 
     reverse = np.zeros((32, 2 * V))
     for r in range(V):
@@ -127,6 +133,7 @@
     return {
         "x_forward": stacked(x_forward),
         "x_inverse": np.stack(x_inverse),
+        "x_slab": np.stack([np.stack(a) for a in x_slab]),
         "plane_forward": chunked(np.stack(split_constant(plane_forward))),
         "plane_inverse": chunked(np.stack(split_constant(plane_inverse))),
         "place": chunked(place.astype(ml_dtypes.bfloat16)),
@@ -136,7 +143,7 @@
     }
 
 
-NAMES = ("x_forward", "x_inverse", "plane_forward", "plane_inverse", "place", "unplace", "reverse", "courants")
+NAMES = ("x_forward", "x_inverse", "plane_forward", "plane_inverse", "place", "unplace", "reverse", "x_slab", "courants")
 
 
 def halves(a):
@@ -163,11 +170,11 @@
 def kernel(
     sizes,
     dist_hbm, kinds_ref, wall_hbm, inflow_hbm, side_hbm, left_hbm, right_hbm, loss_hbm,
-    xf_hbm, xi_hbm, pf_hbm, pi_hbm, place_hbm, unplace_hbm, reverse_hbm, courants_hbm,
+    xf_hbm, xi_hbm, pf_hbm, pi_hbm, place_hbm, unplace_hbm, reverse_hbm, xs_hbm, courants_hbm,
     out_ref,
-    dist, dense, wall, inflow, side, raw, xf, xi, pf, pi, place, unplace, reverse, courants,
-    sides, packed, quads, table, send, recv, field, shaped_hi, shaped_lo, planes, collided, back, own, from_y, from_x,
-    local_sem, send1, recv1, send_own, recv_own, send_y, recv_y, send_x, recv_x, ready,
+    dist, dense, wall, inflow, side, raw, xf, xi, pf, pi, place, unplace, reverse, xs, courants,
+    sides, packed, quads, table, send, recv, field, shaped_hi, shaped_lo, planes, collided, back, own, from_y, from_x, edge, far_raw, far_done,
+    local_sem, send1, recv1, send_own, recv_own, send_y, recv_y, send_x, recv_x, send_raw, recv_raw, ready,
 ):
     n_gx, n_gy = sizes
     gx, gy, me = lax.axis_index("gx"), lax.axis_index("gy"), lax.axis_index("vert")
@@ -175,7 +182,6 @@
     step_y, step_x = 2 * my_y - 1, 2 * my_h - 1
     to_y, to_x = gy + step_y, gx + step_x
     has_y = jnp.logical_and(to_y >= 0, to_y < n_gy)
-    has_x = jnp.logical_and(to_x >= 0, to_x < n_gx)
     core = lax.rem(gx, 2)
     early = lax.rem(gx // 2, 2) == 0
     near_x, far_x = gx + 1 - 2 * core, gx - 1 + 2 * core
@@ -190,7 +196,7 @@
         (left_hbm, raw.at[pl.ds(0, at_gain)]), (right_hbm, raw.at[pl.ds(at_gain, at_gain)]),
         (loss_hbm, raw.at[pl.ds(2 * at_gain, PLANE)]), (place_hbm, place), (reverse_hbm, reverse),
         (xf_hbm, xf), (pf_hbm, pf), (xi_hbm, xi), (pi_hbm, pi), (unplace_hbm, unplace), (side_hbm, side),
-        (courants_hbm.at[me], courants),
+        (courants_hbm.at[me], courants), (xs_hbm.at[me], xs),
     ]
     pulls = [pltpu.make_async_copy(a, b, local_sem.at[i]) for i, (a, b) in enumerate(pulls)]
     for pull in pulls:
@@ -223,13 +229,8 @@
 
     @pl.when(early_far)
     def _():
-        for y in range(2):
-            greet(far_x, gy, y + 2 * (1 - core))
-
-        @pl.when(sends_far)
-        def _():
-            for y in range(2):
-                greet(far_x, gy, y + 2 * core)
+        for v in range(GROUPS):
+            greet(far_x, gy, v)
 
     for i in range(3):
         pulls[i].wait()
@@ -247,9 +248,22 @@
             state = jnp.where(kind == 1, wall[...], jnp.where(kind == 2, inflow[...], own_state))
             send[v, pl.ds(cell * ROWS, ROWS)] = state
     recv[me] = send[me]
+    for y in range(NY):
+        edge[pl.ds(y * ROWS, ROWS)] = send[2 * core + y, pl.ds(0, ROWS)]
+    edge[pl.ds(2 * ROWS, BLOCK - 2 * ROWS)] = jnp.zeros((BLOCK - 2 * ROWS, LANES), F32)
 
     awaited = GROUPS - 1 + jnp.where(has_y, GROUPS, 0) + jnp.where(sends_far, 0, GROUPS)
-    pl.semaphore_wait(barrier, awaited + jnp.where(late_far, jnp.where(sends_far, GROUPS, 2), 0))
+    pl.semaphore_wait(barrier, awaited + jnp.where(late_far, GROUPS, 0))
+
+    push_raw = pltpu.make_async_remote_copy(
+        src_ref=edge, dst_ref=far_raw.at[me], send_sem=send_raw.at[0], recv_sem=recv_raw.at[me],
+        device_id=(far_x, gy, me), device_id_type=MESH,
+    )
+
+    @pl.when(late_far)
+    def _():
+        push_raw.start()
+
     first = []
     for d in range(1, GROUPS):
         to = lax.rem(me + d, GROUPS)
@@ -299,53 +313,61 @@
         pulls[i].wait()
     for d in range(1, GROUPS):
         first[d - 1].wait_recv()
-    for u in range(GROUPS):
-        for c in range(CHUNKS):
-            field[6 * u : 6 * u + 6, c * LANES : (c + 1) * LANES] = recv[u, pl.ds(c, 6, stride=CHUNKS), :]
-    cells = jnp.concatenate([field[:, :PLANE], field[:, PLANE:]], axis=0)
-    hi, lo = halves(cells)
-    along_x = dot(wide(xf, 0, 2, 6 * V), jnp.concatenate([hi, lo, hi], axis=0))
-    hi, lo = halves(along_x)
-    both = jnp.concatenate([hi, lo], axis=0)
-    parts = []
-    for c in range(4):
-        top = dot(both, wide(pf.at[0], 2 * c, 2))
-        parts.append(top[: 2 * V] + top[2 * V :] + dot(hi, wide(pf.at[1], 2 * c, 2)))
-    cc, cs, sc, ss = parts
-    cos_cos, sin_sin = cc, -ss
-    swapped = lambda a: jnp.concatenate([a[V:], -a[:V]], axis=0)
-    spectrum = quadrants(cos_cos, swapped(cs), swapped(sc), sin_sin)
-
-    for t in range(TABLES):
-        at = slice(t * V, (t + 1) * V)
-        a = []
-        for s in range(4):
-            m = table[s, at]
-            a.append(jnp.concatenate([spectrum[s][:V] * m, spectrum[s][V:] * m], axis=0))
-        for c, b in enumerate(quadrants_to_classes(*a)):
-            hi, lo = halves(b)
-            z = dot(wide(xi.at[c], 0, 2, 6 * V), jnp.concatenate([hi, lo, hi], axis=0))
-            hi, lo = halves(z)
-            shaped_hi[c, t * 2 * V : (t + 1) * 2 * V] = hi
-            shaped_lo[c, t * 2 * V : (t + 1) * 2 * V] = lo
-    for c in range(4):
-        top, low = wide(pi.at[0, c], 0, 2), wide(pi.at[1, c], 0, 2)
-        planes[c] = dot(shaped_hi[c], top) + dot(shaped_lo[c], top) + dot(shaped_hi[c], low)
-
-    def fields(t):
-        at = slice(t * 2 * V, (t + 1) * 2 * V)
-        return quadrants(*(planes[c, at] for c in range(4)))
-
-    gain = [0.0] * 4
-    for r in range(RANK):
-        gain = [g + a * b for g, a, b in zip(gain, fields(r), fields(RANK + r))]
-    rates = jnp.concatenate(
-        [jnp.concatenate(list(gain), axis=1), jnp.concatenate(list(fields(2 * RANK)), axis=1)], axis=0
-    )
-    hi, lo = halves(rates)
-    rates = dot(jnp.concatenate([hi, lo], axis=0), wide(unplace, 0, 5, PLANE))
-    rates = rates[: 4 * V] + rates[4 * V :]
-    result = cells + COLLISION_STEP * (rates[: 2 * V] - cells * rates[2 * V :])
+
+    def gather_cells(blocks):
+        for u in range(GROUPS):
+            for c in range(CHUNKS):
+                field[6 * u : 6 * u + 6, c * LANES : (c + 1) * LANES] = blocks[u, pl.ds(c, 6, stride=CHUNKS), :]
+        return jnp.concatenate([field[:, :PLANE], field[:, PLANE:]], axis=0)
+
+    def forward(cells):
+        hi, lo = halves(cells)
+        along_x = dot(wide(xf, 0, 2, 6 * V), jnp.concatenate([hi, lo, hi], axis=0))
+        hi, lo = halves(along_x)
+        both = jnp.concatenate([hi, lo], axis=0)
+        parts = []
+        for c in range(4):
+            top = dot(both, wide(pf.at[0], 2 * c, 2))
+            parts.append(top[: 2 * V] + top[2 * V :] + dot(hi, wide(pf.at[1], 2 * c, 2)))
+        cc, cs, sc, ss = parts
+        swapped = lambda a: jnp.concatenate([a[V:], -a[:V]], axis=0)
+        return quadrants(cc, swapped(cs), swapped(sc), -ss)
+
+    def collide(cells, spectrum, along_x, rows):
+        for t in range(TABLES):
+            at = slice(t * V, (t + 1) * V)
+            a = []
+            for s in range(4):
+                m = table[s, at]
+                a.append(jnp.concatenate([spectrum[s][:V] * m, spectrum[s][V:] * m], axis=0))
+            for c, b in enumerate(quadrants_to_classes(*a)):
+                hi, lo = halves(b)
+                z = dot(wide(along_x.at[c], 0, 2, 6 * V), jnp.concatenate([hi, lo, hi], axis=0))
+                hi, lo = halves(z)
+                shaped_hi[c, t * rows : (t + 1) * rows] = hi
+                shaped_lo[c, t * rows : (t + 1) * rows] = lo
+        used = slice(0, TABLES * rows)
+        for c in range(4):
+            top, low = wide(pi.at[0, c], 0, 2), wide(pi.at[1, c], 0, 2)
+            hi, lo = shaped_hi[c, used], shaped_lo[c, used]
+            planes[c, used] = dot(hi, top) + dot(lo, top) + dot(hi, low)
+
+        def fields(t):
+            return quadrants(*(planes[c, t * rows : (t + 1) * rows] for c in range(4)))
+
+        gain = [0.0] * 4
+        for r in range(RANK):
+            gain = [g + a * b for g, a, b in zip(gain, fields(r), fields(RANK + r))]
+        rates = jnp.concatenate(
+            [jnp.concatenate(list(gain), axis=1), jnp.concatenate(list(fields(2 * RANK)), axis=1)], axis=0
+        )
+        hi, lo = halves(rates)
+        rates = dot(jnp.concatenate([hi, lo], axis=0), wide(unplace, 0, 5, PLANE))
+        rates = rates[: 2 * rows] + rates[2 * rows :]
+        return cells + COLLISION_STEP * (rates[:rows] - cells * rates[rows:])
+
+    cells = gather_cells(recv)
+    result = collide(cells, forward(cells), xi, 2 * V)
     collided[:, :PLANE] = result[:V]
     collided[:, PLANE:] = result[V:]
     for u in range(GROUPS):
@@ -374,7 +396,7 @@
             device_id=(gx, gy, to), device_id_type=MESH,
         )
 
-    @pl.when(jnp.logical_and(has_x, jnp.logical_not(jnp.logical_and(early, sends_far))))
+    @pl.when(jnp.logical_not(sends_far))
     def _():
         for u in range(GROUPS):
             push_x(u).start()
@@ -408,13 +430,49 @@
                     device_id=(gx, to_y, me), device_id_type=MESH,
                 ).wait_recv()
 
-        @pl.when(jnp.logical_and(gx + step >= 0, gx + step < n_gx))
-        def _(k=k):
-            for y in range(2):
-                pltpu.make_async_remote_copy(
-                    src_ref=back.at[0, pl.ds(0, EDGE)], dst_ref=from_x.at[k, y], send_sem=send_x.at[0],
-                    recv_sem=recv_x.at[k, y], device_id=(to_x, gy, me), device_id_type=MESH,
-                ).wait_recv()
+    def wait_x(k):
+        for y in range(2):
+            pltpu.make_async_remote_copy(
+                src_ref=back.at[0, pl.ds(0, EDGE)], dst_ref=from_x.at[k, y], send_sem=send_x.at[0],
+                recv_sem=recv_x.at[k, y], device_id=(near_x, gy, me), device_id_type=MESH,
+            ).wait_recv()
+
+    wait_x(1 - core)
+
+    @pl.when(late_far)
+    def _():
+        wait_x(core)
+
+    def share_raw(d):
+        return pltpu.make_async_remote_copy(
+            src_ref=far_raw.at[me], dst_ref=far_raw.at[me], send_sem=send_raw.at[d], recv_sem=recv_raw.at[me],
+            device_id=(gx, gy, lax.rem(me + d, GROUPS)), device_id_type=MESH,
+        )
+
+    pulls[15].wait()
+
+    @pl.when(early_far)
+    def _():
+        push_raw.wait_recv()
+        for d in range(1, GROUPS):
+            share_raw(d).start()
+        for d in range(1, GROUPS):
+            peer = lax.rem(me + d, GROUPS)
+            pltpu.make_async_remote_copy(
+                src_ref=edge, dst_ref=far_raw.at[peer], send_sem=send_raw.at[d], recv_sem=recv_raw.at[peer],
+                device_id=(gx, gy, peer), device_id_type=MESH,
+            ).wait_recv()
+        spectrum = forward(gather_cells(far_raw))
+        for c in range(CHUNKS):
+            collided[:6, c * LANES : (c + 1) * LANES] = far_raw[me, pl.ds(c, 6, stride=CHUNKS), :]
+        far = jnp.concatenate([collided[:6, :PLANE], collided[:6, PLANE:], jnp.zeros((SOME - 12, PLANE), F32)], axis=0)
+        far = collide(far, spectrum, xs, SOME)
+        collided[:6, :PLANE] = far[:6]
+        collided[:6, PLANE:] = far[6:12]
+        for c in range(CHUNKS):
+            far_done[pl.ds(c, 6, stride=CHUNKS), :] = collided[:6, c * LANES : (c + 1) * LANES]
+        for y in range(NY):
+            from_x[core, y, pl.ds(0, ROWS)] = far_done[pl.ds(y * ROWS, ROWS)]
 
     def at_cell(ref, x):
         cell = (0, 1, 1, 0)[x]
@@ -432,26 +490,39 @@
             above_y = centre[x, 1] if y < 1 else at_cell(from_y.at[1, x // 2], x)
             up_x = jnp.where(higher_x, below_x, above_x)
             up_y = jnp.where(higher_y, below_y, above_y)
-            dense[pl.ds(x * 2 * ROWS + y, ROWS, stride=2), :] = (
+            out_ref[pl.ds(x * 2 * ROWS + y, ROWS, stride=2), :] = (
                 here - courant_x * (here - up_x) - courant_y * (here - up_y)
             )
+
+    for d in range(1, GROUPS):
+        first[d - 1].wait_send()
+        push_own(d).wait_send()
+
+    @pl.when(has_y)
+    def _():
+        for u in range(GROUPS):
+            push_y(u).wait_send()
+
+    @pl.when(jnp.logical_or(jnp.logical_not(sends_far), early_far))
+    def _():
+        for u in range(GROUPS):
+            push_x(u).wait_send()
+
+    @pl.when(late_far)
+    def _():
+        push_raw.wait_send()
+
+    @pl.when(early_far)
+    def _():
+        for d in range(1, GROUPS):
+            share_raw(d).wait_send()
+
+
+def spread(dense, out_ref):
+    for x in range(NX):
         for r in range(ROWS):
             at = (x * ROWS + r) * NY
             out_ref[x, :, r * LANES : (r + 1) * LANES] = dense[at : at + NY, :]
-
-    for d in range(1, GROUPS):
-        first[d - 1].wait_send()
-        push_own(d).wait_send()
-
-    @pl.when(has_y)
-    def _():
-        for u in range(GROUPS):
-            push_y(u).wait_send()
-
-    @pl.when(has_x)
-    def _():
-        for u in range(GROUPS):
-            push_x(u).wait_send()
 
 
 def quadrants_to_classes(pp, pm, mp, mm):
@@ -484,8 +555,8 @@
         pltpu.VMEM((ROWS, LANES), F32),
         pltpu.VMEM((2, SLAB), jnp.int32),
         pltpu.VMEM((TABLES * PLANE, V), F32),
-        *(pltpu.VMEM(t.shape, t.dtype) for t in tables[:-1]),
-        pltpu.VMEM(tables[-1].shape[1:], F32),
+        *(pltpu.VMEM(t.shape, t.dtype) for t in tables[:-2]),
+        *(pltpu.VMEM(t.shape[1:], t.dtype) for t in tables[-2:]),
         pltpu.VMEM((2, ROWS, LANES), jnp.int32),
         pltpu.VMEM((TABLES * V, GROUPED), F32),
         pltpu.VMEM((4, TABLES * V, W), F32),
@@ -501,16 +572,20 @@
         pltpu.VMEM((GROUPS, BLOCK, LANES), F32),
         pltpu.VMEM((2, 2, BLOCK, LANES), F32),
         pltpu.VMEM((2, 2, EDGE, LANES), F32),
-        dma((15,)),
+        pltpu.VMEM((BLOCK, LANES), F32),
+        pltpu.VMEM((GROUPS, BLOCK, LANES), F32),
+        pltpu.VMEM((BLOCK, LANES), F32),
+        dma((16,)),
         dma((GROUPS,)), dma((GROUPS,)),
         dma((GROUPS,)), dma((GROUPS,)),
         dma((GROUPS,)), dma((2, 2)),
         dma((GROUPS,)), dma((2, 2)),
+        dma((GROUPS,)), dma((GROUPS,)),
         pltpu.SemaphoreType.REGULAR,
     ]
-    return pl.pallas_call(
+    dense = pl.pallas_call(
         functools.partial(kernel, sizes),
-        out_shape=jax.ShapeDtypeStruct((NX, NY, SLAB), F32),
+        out_shape=pltpu.VMEM((NX * NY * ROWS, LANES), F32),
         in_specs=spaces,
         out_specs=pl.BlockSpec(memory_space=pltpu.VMEM),
         scratch_shapes=held,
@@ -520,6 +595,13 @@
         cost_estimate=pl.CostEstimate(flops=3_000_000_000, bytes_accessed=10_000_000, transcendentals=0),
         name="step",
     )(*operands)
+    return pl.pallas_call(
+        spread,
+        out_shape=jax.ShapeDtypeStruct((NX, NY, SLAB), F32),
+        in_specs=[pl.BlockSpec(memory_space=pltpu.VMEM)],
+        out_specs=pl.BlockSpec(memory_space=pltpu.VMEM),
+        name="spread",
+    )(pltpu.with_memory_space_constraint(dense, pltpu.VMEM))
 
 
 def solution(mesh):

time: 30.3 us -> 27.3 us (0.901)
  local copies, waits for them, and re-layouts: 1.55 us -> 0 us
  Pallas kernels: 28.6 us -> 27.2 us
    unnamed x1 -> x0, local copies, waits for them, and re-layouts: 1.55 us -> none
    pallas_call x1 -> x2, Pallas kernels: 28.6 us -> 27.2 us  [the longest x1 26.5 us: on_device(): pl.pallas_call(functools.partial(kernel, sizes), out_shape=pltpu.VMEM((NX...]
where the time goes in v3:
time: 27.3 us; the launch traced here: 27.2 us
  Pallas kernels  27.2 us (100%)
    pallas_call x1, Pallas kernels, on_device(): pl.pallas_call(functools.partial(kernel, sizes), out_shape=pltpu.VMEM((NX...  26.5 us
    pallas_call x1, Pallas kernels, on_device(): pl.pallas_call(spread, out_shape=jax.ShapeDtypeStruct((NX, NY, SLAB), F32...  0.65 us

profile of v3, /device:TPU:1, one launch (start us, length us, event | category | flops | bytes accessed | tf_op | source)
XLA Modules:
  0.0 27.2 jit_solution(12852704627647269596)
XLA Ops:
  0.0 26.5 %step.1.dense = f32[216,128]{1,0:T(8,128)S(1)} custom-call(f32[4,2,3456]{2,1,0:T(2,128)} %dist_hbm.1, s32[2,4]{1,0:T(2,128)} %bitcast.11, f32[27,128]{1,0:T(8,128)} %bitcast.9, f32[27,128]{1,0:T(8,128)} %bitcast.10, s32[2,3456]{1,0:T(2,128)} %side_hbm.1, f32[2304,24]{1,0:T(8,128)} %bitcast.6, f32[2304,24]{1,0:T(8,128)} %bitcast.7, f32[576,24]{1,0:T(8,128)} %bitcast.8, ...), custom_call_target="tpu_custom_call" | custom-call | flops 3000000000 | bytes 10000000 | tf_op jit(solution)/shard_map/step/pallas_call | solution.py:586
  26.5 0.7 %spread.1 = f32[4,2,3456]{2,1,0:T(2,128)} custom-call(f32[216,128]{1,0:T(8,128)S(1)} %step.1.dense), custom_call_target="tpu_custom_call" | custom-call | tf_op jit(solution)/shard_map/spread/pallas_call | solution.py:598

commit v4 on v3

--- a/solution.py
+++ b/solution.py
@@ -169,10 +169,10 @@
 
 def kernel(
     sizes,
-    dist_hbm, kinds_ref, wall_hbm, inflow_hbm, side_hbm, left_hbm, right_hbm, loss_hbm,
+    dist_hbm, kinds_hbm, wall_hbm, inflow_hbm, side_hbm, left_hbm, right_hbm, loss_hbm,
     xf_hbm, xi_hbm, pf_hbm, pi_hbm, place_hbm, unplace_hbm, reverse_hbm, xs_hbm, courants_hbm,
     out_ref,
-    dist, dense, wall, inflow, side, raw, xf, xi, pf, pi, place, unplace, reverse, xs, courants,
+    dist, dense, kinds, wall, inflow, side, raw, xf, xi, pf, pi, place, unplace, reverse, xs, courants,
     sides, packed, quads, table, send, recv, field, shaped_hi, shaped_lo, planes, collided, back, own, from_y, from_x, edge, far_raw, far_done,
     local_sem, send1, recv1, send_own, recv_own, send_y, recv_y, send_x, recv_x, send_raw, recv_raw, ready,
 ):
@@ -190,31 +190,15 @@
     early_far = jnp.logical_and(has_far, early)
     late_far = jnp.logical_and(has_far, jnp.logical_not(early))
 
-    at_gain = RANK * V * PLANE // V
-    pulls = [
-        (dist_hbm, dist), (wall_hbm, wall), (inflow_hbm, inflow),
-        (left_hbm, raw.at[pl.ds(0, at_gain)]), (right_hbm, raw.at[pl.ds(at_gain, at_gain)]),
-        (loss_hbm, raw.at[pl.ds(2 * at_gain, PLANE)]), (place_hbm, place), (reverse_hbm, reverse),
-        (xf_hbm, xf), (pf_hbm, pf), (xi_hbm, xi), (pi_hbm, pi), (unplace_hbm, unplace), (side_hbm, side),
-        (courants_hbm.at[me], courants), (xs_hbm.at[me], xs),
-    ]
-    pulls = [pltpu.make_async_copy(a, b, local_sem.at[i]) for i, (a, b) in enumerate(pulls)]
-    for pull in pulls:
-        pull.start()
-
-    for k in range(2):
-        @pl.when(gx == k * (n_gx - 1))
-        def _(k=k):
-            from_x[k] = jnp.zeros((2, EDGE, LANES), F32)
-
-        @pl.when(gy == k * (n_gy - 1))
-        def _(k=k):
-            from_y[k] = jnp.zeros((2, BLOCK, LANES), F32)
-
     barrier = pltpu.get_barrier_semaphore()
 
     def greet(x, y, v):
         pl.semaphore_signal(barrier, inc=1, device_id=(x, y, v), device_id_type=MESH)
+
+    @pl.when(early_far)
+    def _():
+        for v in range(GROUPS):
+            greet(far_x, gy, v)
 
     for d in range(1, GROUPS):
         greet(gx, gy, lax.rem(me + d, GROUPS))
@@ -227,12 +211,28 @@
     for y in range(2):
         greet(near_x, gy, y + 2 * core)
 
-    @pl.when(early_far)
-    def _():
-        for v in range(GROUPS):
-            greet(far_x, gy, v)
-
-    for i in range(3):
+    at_gain = RANK * V * PLANE // V
+    pulls = [
+        (dist_hbm, dist), (wall_hbm, wall), (inflow_hbm, inflow),
+        (left_hbm, raw.at[pl.ds(0, at_gain)]), (right_hbm, raw.at[pl.ds(at_gain, at_gain)]),
+        (loss_hbm, raw.at[pl.ds(2 * at_gain, PLANE)]), (place_hbm, place), (reverse_hbm, reverse),
+        (xf_hbm, xf), (pf_hbm, pf), (xi_hbm, xi), (pi_hbm, pi), (unplace_hbm, unplace), (side_hbm, side),
+        (courants_hbm.at[me], courants), (xs_hbm.at[me], xs), (kinds_hbm, kinds),
+    ]
+    pulls = [pltpu.make_async_copy(a, b, local_sem.at[i]) for i, (a, b) in enumerate(pulls)]
+    for i in (0, 16, 1, 2, *range(3, 16)):
+        pulls[i].start()
+
+    @pl.when(jnp.logical_not(late_far))
+    def _():
+        from_x[core] = jnp.zeros((2, EDGE, LANES), F32)
+
+    for k in range(2):
+        @pl.when(gy == k * (n_gy - 1))
+        def _(k=k):
+            from_y[k] = jnp.zeros((2, BLOCK, LANES), F32)
+
+    for i in (0, 1, 2, 16):
         pulls[i].wait()
     for x in range(NX):
         for r in range(ROWS):
@@ -243,7 +243,7 @@
         send[v, pl.ds(48, 8)] = jnp.zeros((8, LANES), F32)
         for cell in range(2):
             x = 3 * h + (1 - 2 * h) * cell
-            kind = jnp.full((ROWS, LANES), kinds_ref[y, x], jnp.int32)
+            kind = jnp.broadcast_to(kinds[y : y + 1, x : x + 1], (ROWS, LANES))
             own_state = dense[pl.ds(x * 2 * ROWS + y, ROWS, stride=2), :]
             state = jnp.where(kind == 1, wall[...], jnp.where(kind == 2, inflow[...], own_state))
             send[v, pl.ds(cell * ROWS, ROWS)] = state
@@ -255,14 +255,31 @@
     awaited = GROUPS - 1 + jnp.where(has_y, GROUPS, 0) + jnp.where(sends_far, 0, GROUPS)
     pl.semaphore_wait(barrier, awaited + jnp.where(late_far, GROUPS, 0))
 
-    push_raw = pltpu.make_async_remote_copy(
-        src_ref=edge, dst_ref=far_raw.at[me], send_sem=send_raw.at[0], recv_sem=recv_raw.at[me],
-        device_id=(far_x, gy, me), device_id_type=MESH,
-    )
+    every = gy == n_gy // 8
+    some = jnp.logical_or(every, gy < n_gy // 8)
+
+    def push_raw(d):
+        return pltpu.make_async_remote_copy(
+            src_ref=edge, dst_ref=far_raw.at[me], send_sem=send_raw.at[d], recv_sem=recv_raw.at[me],
+            device_id=(far_x, gy, lax.rem(me + d, GROUPS)), device_id_type=MESH,
+        )
+
+    def at_offsets(near, across, act):
+        @pl.when(near)
+        def _():
+            for d in (1, 3):
+                act(d)
+
+        @pl.when(across)
+        def _():
+            act(2)
+
+    unshared = jnp.logical_not(every), jnp.logical_not(some)
 
     @pl.when(late_far)
     def _():
-        push_raw.start()
+        push_raw(0).start()
+        at_offsets(every, some, lambda d: push_raw(d).start())
 
     first = []
     for d in range(1, GROUPS):
@@ -410,11 +427,25 @@
         push_own(d).start()
     own[me] = back[me]
 
-    @pl.when(jnp.logical_and(early_far, sends_far))
-    def _():
+    def push_far():
         pl.semaphore_wait(ready, GROUPS)
         for u in range(GROUPS):
             push_x(u).start()
+
+    @pl.when(jnp.logical_and(early_far, sends_far))
+    def _():
+        push_far()
+
+    def share_raw(d):
+        return pltpu.make_async_remote_copy(
+            src_ref=far_raw.at[me], dst_ref=far_raw.at[me], send_sem=send_raw.at[d], recv_sem=recv_raw.at[me],
+            device_id=(gx, gy, lax.rem(me + d, GROUPS)), device_id_type=MESH,
+        )
+
+    @pl.when(early_far)
+    def _():
+        push_raw(0).wait_recv()
+        at_offsets(*unshared, lambda d: share_raw(d).start())
 
     pulls[14].wait()
     for d in range(1, GROUPS):
@@ -443,19 +474,30 @@
     def _():
         wait_x(core)
 
-    def share_raw(d):
-        return pltpu.make_async_remote_copy(
-            src_ref=far_raw.at[me], dst_ref=far_raw.at[me], send_sem=send_raw.at[d], recv_sem=recv_raw.at[me],
-            device_id=(gx, gy, lax.rem(me + d, GROUPS)), device_id_type=MESH,
-        )
+    def at_cell(ref, x):
+        cell = (0, 1, 1, 0)[x]
+        return ref[pl.ds(cell * ROWS, ROWS), :]
+
+    courant_x, courant_y = courants[0, pl.ds(0, ROWS)], courants[1, pl.ds(0, ROWS)]
+    higher_x, higher_y = sides[0] == 1, sides[1] == 1
+    centre = {(x, y): at_cell(own.at[y + 2 * (x // 2)], x) for x in range(NX) for y in range(NY)}
+    for x in range(NX):
+        for y in range(NY):
+            here = centre[x, y]
+            below_x = centre[x - 1, y] if x > 0 else from_x[0, y, pl.ds(0, ROWS)]
+            above_x = centre[x + 1, y] if x < NX - 1 else from_x[1, y, pl.ds(0, ROWS)]
+            below_y = centre[x, 0] if y > 0 else at_cell(from_y.at[0, x // 2], x)
+            above_y = centre[x, 1] if y < 1 else at_cell(from_y.at[1, x // 2], x)
+            up_x = jnp.where(higher_x, below_x, above_x)
+            up_y = jnp.where(higher_y, below_y, above_y)
+            out_ref[pl.ds(x * 2 * ROWS + y, ROWS, stride=2), :] = (
+                here - courant_x * (here - up_x) - courant_y * (here - up_y)
+            )
 
     pulls[15].wait()
 
     @pl.when(early_far)
     def _():
-        push_raw.wait_recv()
-        for d in range(1, GROUPS):
-            share_raw(d).start()
         for d in range(1, GROUPS):
             peer = lax.rem(me + d, GROUPS)
             pltpu.make_async_remote_copy(
@@ -471,28 +513,11 @@
         collided[:6, PLANE:] = far[6:12]
         for c in range(CHUNKS):
             far_done[pl.ds(c, 6, stride=CHUNKS), :] = collided[:6, c * LANES : (c + 1) * LANES]
+        x = (NX - 1) * core
         for y in range(NY):
-            from_x[core, y, pl.ds(0, ROWS)] = far_done[pl.ds(y * ROWS, ROWS)]
-
-    def at_cell(ref, x):
-        cell = (0, 1, 1, 0)[x]
-        return ref[pl.ds(cell * ROWS, ROWS), :]
-
-    courant_x, courant_y = courants[0, pl.ds(0, ROWS)], courants[1, pl.ds(0, ROWS)]
-    higher_x, higher_y = sides[0] == 1, sides[1] == 1
-    centre = {(x, y): at_cell(own.at[y + 2 * (x // 2)], x) for x in range(NX) for y in range(NY)}
-    for x in range(NX):
-        for y in range(NY):
-            here = centre[x, y]
-            below_x = centre[x - 1, y] if x > 0 else from_x[0, y, pl.ds(0, ROWS)]
-            above_x = centre[x + 1, y] if x < NX - 1 else from_x[1, y, pl.ds(0, ROWS)]
-            below_y = centre[x, 0] if y > 0 else at_cell(from_y.at[0, x // 2], x)
-            above_y = centre[x, 1] if y < 1 else at_cell(from_y.at[1, x // 2], x)
-            up_x = jnp.where(higher_x, below_x, above_x)
-            up_y = jnp.where(higher_y, below_y, above_y)
-            out_ref[pl.ds(x * 2 * ROWS + y, ROWS, stride=2), :] = (
-                here - courant_x * (here - up_x) - courant_y * (here - up_y)
-            )
+            at = pl.ds(x * NY * ROWS + y, ROWS, stride=NY)
+            inward = courant_x * far_done[pl.ds(y * ROWS, ROWS)]
+            out_ref[at, :] = out_ref[at, :] + jnp.where(sides[0] == 1 - core, inward, 0.0)
 
     for d in range(1, GROUPS):
         first[d - 1].wait_send()
@@ -510,12 +535,12 @@
 
     @pl.when(late_far)
     def _():
-        push_raw.wait_send()
+        push_raw(0).wait_send()
+        at_offsets(every, some, lambda d: push_raw(d).wait_send())
 
     @pl.when(early_far)
     def _():
-        for d in range(1, GROUPS):
-            share_raw(d).wait_send()
+        at_offsets(*unshared, lambda d: share_raw(d).wait_send())
 
 
 def spread(dense, out_ref):
@@ -546,11 +571,11 @@
         *tables,
     ]
     spaces = [pl.BlockSpec(memory_space=pl.ANY)] * len(operands)
-    spaces[1] = pl.BlockSpec(memory_space=pltpu.SMEM)
     dma = pltpu.SemaphoreType.DMA
     held = [
         pltpu.VMEM((NX, NY, SLAB), F32),
         pltpu.VMEM((NX * NY * ROWS, LANES), F32),
+        pltpu.VMEM((NY, NX), jnp.int32),
         pltpu.VMEM((ROWS, LANES), F32),
         pltpu.VMEM((ROWS, LANES), F32),
         pltpu.VMEM((2, SLAB), jnp.int32),
@@ -575,7 +600,7 @@
         pltpu.VMEM((BLOCK, LANES), F32),
         pltpu.VMEM((GROUPS, BLOCK, LANES), F32),
         pltpu.VMEM((BLOCK, LANES), F32),
-        dma((16,)),
+        dma((17,)),
         dma((GROUPS,)), dma((GROUPS,)),
         dma((GROUPS,)), dma((GROUPS,)),
         dma((GROUPS,)), dma((2, 2)),

time: 27.3 us -> 26.2 us (0.960)
  Pallas kernels: 27.2 us -> 26.1 us
    pallas_call x1, Pallas kernels: 26.5 us -> 25.4 us  [on_device(): pl.pallas_call(functools.partial(kernel, sizes), out_shape=pltpu.VMEM((NX...]
where the time goes in v4:
time: 26.2 us; the launch traced here: 26.1 us
  Pallas kernels  26.1 us (100%)
    pallas_call x1, Pallas kernels, on_device(): pl.pallas_call(functools.partial(kernel, sizes), out_shape=pltpu.VMEM((NX...  25.4 us
    pallas_call x1, Pallas kernels, on_device(): pl.pallas_call(spread, out_shape=jax.ShapeDtypeStruct((NX, NY, SLAB), F32...  0.65 us

profile of v4, /device:TPU:1, one launch (start us, length us, event | category | flops | bytes accessed | tf_op | source)
XLA Modules:
  0.0 26.1 jit_solution(6087298378565715672)
XLA Ops:
  0.0 25.4 %step.1.dense = f32[216,128]{1,0:T(8,128)S(1)} custom-call(f32[4,2,3456]{2,1,0:T(2,128)} %dist_hbm.1, s32[2,4]{1,0:T(2,128)} %bitcast.11, f32[27,128]{1,0:T(8,128)} %bitcast.9, f32[27,128]{1,0:T(8,128)} %bitcast.10, s32[2,3456]{1,0:T(2,128)} %side_hbm.1, f32[2304,24]{1,0:T(8,128)} %bitcast.6, f32[2304,24]{1,0:T(8,128)} %bitcast.7, f32[576,24]{1,0:T(8,128)} %bitcast.8, ...), custom_call_target="tpu_custom_call" | custom-call | flops 3000000000 | bytes 10000000 | tf_op jit(solution)/shard_map/step/pallas_call | solution.py:611
  25.4 0.7 %spread.1 = f32[4,2,3456]{2,1,0:T(2,128)} custom-call(f32[216,128]{1,0:T(8,128)S(1)} %step.1.dense), custom_call_target="tpu_custom_call" | custom-call | tf_op jit(solution)/shard_map/spread/pallas_call | solution.py:623

commit v5 on v4

--- a/solution.py
+++ b/solution.py
@@ -255,8 +255,8 @@
     awaited = GROUPS - 1 + jnp.where(has_y, GROUPS, 0) + jnp.where(sends_far, 0, GROUPS)
     pl.semaphore_wait(barrier, awaited + jnp.where(late_far, GROUPS, 0))
 
-    every = gy == n_gy // 8
-    some = jnp.logical_or(every, gy < n_gy // 8)
+    receiver = jnp.where(early, core, 1 - core)
+    every = jnp.logical_or(gy == n_gy // 8, jnp.logical_and(gy < n_gy // 8, receiver == 1))
 
     def push_raw(d):
         return pltpu.make_async_remote_copy(
@@ -264,22 +264,18 @@
             device_id=(far_x, gy, lax.rem(me + d, GROUPS)), device_id_type=MESH,
         )
 
-    def at_offsets(near, across, act):
-        @pl.when(near)
+    def at_others(wanted, act):
+        @pl.when(wanted)
         def _():
-            for d in (1, 3):
+            for d in range(1, GROUPS):
                 act(d)
 
-        @pl.when(across)
-        def _():
-            act(2)
-
-    unshared = jnp.logical_not(every), jnp.logical_not(some)
+    shared = jnp.logical_not(every)
 
     @pl.when(late_far)
     def _():
         push_raw(0).start()
-        at_offsets(every, some, lambda d: push_raw(d).start())
+        at_others(every, lambda d: push_raw(d).start())
 
     first = []
     for d in range(1, GROUPS):
@@ -445,7 +441,7 @@
     @pl.when(early_far)
     def _():
         push_raw(0).wait_recv()
-        at_offsets(*unshared, lambda d: share_raw(d).start())
+        at_others(shared, lambda d: share_raw(d).start())
 
     pulls[14].wait()
     for d in range(1, GROUPS):
@@ -536,11 +532,11 @@
     @pl.when(late_far)
     def _():
         push_raw(0).wait_send()
-        at_offsets(every, some, lambda d: push_raw(d).wait_send())
+        at_others(every, lambda d: push_raw(d).wait_send())
 
     @pl.when(early_far)
     def _():
-        at_offsets(*unshared, lambda d: share_raw(d).wait_send())
+        at_others(shared, lambda d: share_raw(d).wait_send())
 
 
 def spread(dense, out_ref):

time: 26.2 us -> 25.6 us (0.977); the launches traced: 26.1 us -> 25.1 us
  Pallas kernels: 26.1 us -> 25.1 us
    pallas_call x1, Pallas kernels: 25.4 us -> 24.5 us  [on_device(): pl.pallas_call(functools.partial(kernel, sizes), out_shape=pltpu.VMEM((NX...]
where the time goes in v5:
time: 25.6 us; the launch traced here: 25.1 us
  Pallas kernels  25.1 us (98%)
    pallas_call x1, Pallas kernels, on_device(): pl.pallas_call(functools.partial(kernel, sizes), out_shape=pltpu.VMEM((NX...  24.5 us
    pallas_call x1, Pallas kernels, on_device(): pl.pallas_call(spread, out_shape=jax.ShapeDtypeStruct((NX, NY, SLAB), F32...  0.65 us

profile of v5, /device:TPU:1, one launch (start us, length us, event | category | flops | bytes accessed | tf_op | source)
XLA Modules:
  0.0 25.1 jit_solution(12802912307003064717)
XLA Ops:
  0.0 24.5 %step.1.dense = f32[216,128]{1,0:T(8,128)S(1)} custom-call(f32[4,2,3456]{2,1,0:T(2,128)} %dist_hbm.1, s32[2,4]{1,0:T(2,128)} %bitcast.11, f32[27,128]{1,0:T(8,128)} %bitcast.9, f32[27,128]{1,0:T(8,128)} %bitcast.10, s32[2,3456]{1,0:T(2,128)} %side_hbm.1, f32[2304,24]{1,0:T(8,128)} %bitcast.6, f32[2304,24]{1,0:T(8,128)} %bitcast.7, f32[576,24]{1,0:T(8,128)} %bitcast.8, ...), custom_call_target="tpu_custom_call" | custom-call | flops 3000000000 | bytes 10000000 | tf_op jit(solution)/shard_map/step/pallas_call | solution.py:607
  24.5 0.7 %spread.1 = f32[4,2,3456]{2,1,0:T(2,128)} custom-call(f32[216,128]{1,0:T(8,128)S(1)} %step.1.dense), custom_call_target="tpu_custom_call" | custom-call | tf_op jit(solution)/shard_map/spread/pallas_call | solution.py:619

commit v6 on v5

--- a/solution.py
+++ b/solution.py
@@ -32,6 +32,7 @@
 PACK = 5
 GROUPED = 5 * LANES
 SIGNS = ((1, 1), (1, -1), (-1, 1), (-1, -1))
+OTHERS = (2, 1, 3)
 COLLISION_STEP = 0.25
 COURANT = 0.45
 
@@ -200,7 +201,7 @@
         for v in range(GROUPS):
             greet(far_x, gy, v)
 
-    for d in range(1, GROUPS):
+    for d in OTHERS:
         greet(gx, gy, lax.rem(me + d, GROUPS))
     for step in (-1, 1):
         @pl.when(jnp.logical_and(gy + step >= 0, gy + step < n_gy))
@@ -267,7 +268,7 @@
     def at_others(wanted, act):
         @pl.when(wanted)
         def _():
-            for d in range(1, GROUPS):
+            for d in OTHERS:
                 act(d)
 
     shared = jnp.logical_not(every)
@@ -278,7 +279,7 @@
         at_others(every, lambda d: push_raw(d).start())
 
     first = []
-    for d in range(1, GROUPS):
+    for d in OTHERS:
         to = lax.rem(me + d, GROUPS)
         first.append(
             pltpu.make_async_remote_copy(
@@ -419,7 +420,7 @@
         for u in range(GROUPS):
             push_y(u).start()
 
-    for d in range(1, GROUPS):
+    for d in OTHERS:
         push_own(d).start()
     own[me] = back[me]
 
@@ -490,6 +491,25 @@
                 here - courant_x * (here - up_x) - courant_y * (here - up_y)
             )
 
+    for d in range(1, GROUPS):
+        first[d - 1].wait_send()
+        push_own(d).wait_send()
+
+    @pl.when(has_y)
+    def _():
+        for u in range(GROUPS):
+            push_y(u).wait_send()
+
+    @pl.when(jnp.logical_or(jnp.logical_not(sends_far), early_far))
+    def _():
+        for u in range(GROUPS):
+            push_x(u).wait_send()
+
+    @pl.when(late_far)
+    def _():
+        push_raw(0).wait_send()
+        at_others(every, lambda d: push_raw(d).wait_send())
+
     pulls[15].wait()
 
     @pl.when(early_far)
@@ -500,6 +520,7 @@
                 src_ref=edge, dst_ref=far_raw.at[peer], send_sem=send_raw.at[d], recv_sem=recv_raw.at[peer],
                 device_id=(gx, gy, peer), device_id_type=MESH,
             ).wait_recv()
+        at_others(shared, lambda d: share_raw(d).wait_send())
         spectrum = forward(gather_cells(far_raw))
         for c in range(CHUNKS):
             collided[:6, c * LANES : (c + 1) * LANES] = far_raw[me, pl.ds(c, 6, stride=CHUNKS), :]
@@ -514,29 +535,6 @@
             at = pl.ds(x * NY * ROWS + y, ROWS, stride=NY)
             inward = courant_x * far_done[pl.ds(y * ROWS, ROWS)]
             out_ref[at, :] = out_ref[at, :] + jnp.where(sides[0] == 1 - core, inward, 0.0)
-
-    for d in range(1, GROUPS):
-        first[d - 1].wait_send()
-        push_own(d).wait_send()
-
-    @pl.when(has_y)
-    def _():
-        for u in range(GROUPS):
-            push_y(u).wait_send()
-
-    @pl.when(jnp.logical_or(jnp.logical_not(sends_far), early_far))
-    def _():
-        for u in range(GROUPS):
-            push_x(u).wait_send()
-
-    @pl.when(late_far)
-    def _():
-        push_raw(0).wait_send()
-        at_others(every, lambda d: push_raw(d).wait_send())
-
-    @pl.when(early_far)
-    def _():
-        at_others(shared, lambda d: share_raw(d).wait_send())
 
 
 def spread(dense, out_ref):

time: 25.6 us -> 25.4 us (level)
  no operation moved by 1% of the time
where the time goes in v6:
time: 25.4 us; the launch traced here: 25.1 us
  Pallas kernels  25.1 us (99%)
    pallas_call x1, Pallas kernels, on_device(): pl.pallas_call(functools.partial(kernel, sizes), out_shape=pltpu.VMEM((NX...  24.5 us
    pallas_call x1, Pallas kernels, on_device(): pl.pallas_call(spread, out_shape=jax.ShapeDtypeStruct((NX, NY, SLAB), F32...  0.65 us

profile of v6, /device:TPU:1, one launch (start us, length us, event | category | flops | bytes accessed | tf_op | source)
XLA Modules:
  0.0 25.1 jit_solution(11937334629622595047)
XLA Ops:
  0.0 24.5 %step.1.dense = f32[216,128]{1,0:T(8,128)S(1)} custom-call(f32[4,2,3456]{2,1,0:T(2,128)} %dist_hbm.1, s32[2,4]{1,0:T(2,128)} %bitcast.11, f32[27,128]{1,0:T(8,128)} %bitcast.9, f32[27,128]{1,0:T(8,128)} %bitcast.10, s32[2,3456]{1,0:T(2,128)} %side_hbm.1, f32[2304,24]{1,0:T(8,128)} %bitcast.6, f32[2304,24]{1,0:T(8,128)} %bitcast.7, f32[576,24]{1,0:T(8,128)} %bitcast.8, ...), custom_call_target="tpu_custom_call" | custom-call | flops 3000000000 | bytes 10000000 | tf_op jit(solution)/shard_map/step/pallas_call | solution.py:605
  24.5 0.7 %spread.1 = f32[4,2,3456]{2,1,0:T(2,128)} custom-call(f32[216,128]{1,0:T(8,128)S(1)} %step.1.dense), custom_call_target="tpu_custom_call" | custom-call | tf_op jit(solution)/shard_map/spread/pallas_call | solution.py:617

commit v7 on v6

--- a/solution.py
+++ b/solution.py
@@ -348,6 +348,7 @@
         return quadrants(cc, swapped(cs), swapped(sc), -ss)
 
     def collide(cells, spectrum, along_x, rows):
+        lanes = (W, W, W, LANES)
         for t in range(TABLES):
             at = slice(t * V, (t + 1) * V)
             a = []
@@ -355,19 +356,23 @@
                 m = table[s, at]
                 a.append(jnp.concatenate([spectrum[s][:V] * m, spectrum[s][V:] * m], axis=0))
             for c, b in enumerate(quadrants_to_classes(*a)):
-                hi, lo = halves(b)
+                hi, lo = halves(b[:, : lanes[c]])
                 z = dot(wide(along_x.at[c], 0, 2, 6 * V), jnp.concatenate([hi, lo, hi], axis=0))
                 hi, lo = halves(z)
-                shaped_hi[c, t * rows : (t + 1) * rows] = hi
-                shaped_lo[c, t * rows : (t + 1) * rows] = lo
+                shaped_hi[c, t * rows : (t + 1) * rows, : lanes[c]] = hi
+                shaped_lo[c, t * rows : (t + 1) * rows, : lanes[c]] = lo
         used = slice(0, TABLES * rows)
         for c in range(4):
-            top, low = wide(pi.at[0, c], 0, 2), wide(pi.at[1, c], 0, 2)
-            hi, lo = shaped_hi[c, used], shaped_lo[c, used]
-            planes[c, used] = dot(hi, top) + dot(lo, top) + dot(hi, low)
+            n = lanes[c]
+            top, low = (wide(pi.at[k, c, :, pl.ds(0, n)], 0, n // LANES) for k in range(2))
+            hi, lo = shaped_hi[c, used, :n], shaped_lo[c, used, :n]
+            planes[c, used, :n] = dot(hi, top) + dot(lo, top) + dot(hi, low)
 
         def fields(t):
-            return quadrants(*(planes[c, t * rows : (t + 1) * rows] for c in range(4)))
+            at = slice(t * rows, (t + 1) * rows)
+            parts = [planes[c, at, : lanes[c]] for c in range(4)]
+            parts[3] = jnp.concatenate([parts[3], jnp.zeros((rows, W - LANES), F32)], axis=1)
+            return quadrants(*parts)
 
         gain = [0.0] * 4
         for r in range(RANK):

time: 25.4 us -> 25.4 us (level)
  no operation moved by 1% of the time
where the time goes in v7:
time: 25.4 us; the launch traced here: 25.1 us
  Pallas kernels  25.1 us (99%)
    pallas_call x1, Pallas kernels, on_device(): pl.pallas_call(functools.partial(kernel, sizes), out_shape=pltpu.VMEM((NX...  24.4 us
    pallas_call x1, Pallas kernels, on_device(): pl.pallas_call(spread, out_shape=jax.ShapeDtypeStruct((NX, NY, SLAB), F32...  0.65 us

profile of v7, /device:TPU:1, one launch (start us, length us, event | category | flops | bytes accessed | tf_op | source)
XLA Modules:
  0.0 25.1 jit_solution(108562673683722850)
XLA Ops:
  0.0 24.4 %step.1.dense = f32[216,128]{1,0:T(8,128)S(1)} custom-call(f32[4,2,3456]{2,1,0:T(2,128)} %dist_hbm.1, s32[2,4]{1,0:T(2,128)} %bitcast.11, f32[27,128]{1,0:T(8,128)} %bitcast.9, f32[27,128]{1,0:T(8,128)} %bitcast.10, s32[2,3456]{1,0:T(2,128)} %side_hbm.1, f32[2304,24]{1,0:T(8,128)} %bitcast.6, f32[2304,24]{1,0:T(8,128)} %bitcast.7, f32[576,24]{1,0:T(8,128)} %bitcast.8, ...), custom_call_target="tpu_custom_call" | custom-call | flops 3000000000 | bytes 10000000 | tf_op jit(solution)/shard_map/step/pallas_call | solution.py:610
  24.4 0.7 %spread.1 = f32[4,2,3456]{2,1,0:T(2,128)} custom-call(f32[216,128]{1,0:T(8,128)S(1)} %step.1.dense), custom_call_target="tpu_custom_call" | custom-call | tf_op jit(solution)/shard_map/spread/pallas_call | solution.py:622

commit v8 on v7

--- a/solution.py
+++ b/solution.py
@@ -201,8 +201,6 @@
         for v in range(GROUPS):
             greet(far_x, gy, v)
 
-    for d in OTHERS:
-        greet(gx, gy, lax.rem(me + d, GROUPS))
     for step in (-1, 1):
         @pl.when(jnp.logical_and(gy + step >= 0, gy + step < n_gy))
         def _(step=step):
@@ -211,6 +209,8 @@
 
     for y in range(2):
         greet(near_x, gy, y + 2 * core)
+    for d in OTHERS:
+        greet(gx, gy, lax.rem(me + d, GROUPS))
 
     at_gain = RANK * V * PLANE // V
     pulls = [

time: 25.4 us -> 25.4 us (level)
  no operation moved by 1% of the time
where the time goes in v8:
time: 25.4 us; the launch traced here: 25.1 us
  Pallas kernels  25.1 us (99%)
    pallas_call x1, Pallas kernels, on_device(): pl.pallas_call(functools.partial(kernel, sizes), out_shape=pltpu.VMEM((NX...  24.4 us
    pallas_call x1, Pallas kernels, on_device(): pl.pallas_call(spread, out_shape=jax.ShapeDtypeStruct((NX, NY, SLAB), F32...  0.65 us

profile of v8, /device:TPU:1, one launch (start us, length us, event | category | flops | bytes accessed | tf_op | source)
XLA Modules:
  0.0 25.1 jit_solution(15863102282687595897)
XLA Ops:
  0.0 24.4 %step.1.dense = f32[216,128]{1,0:T(8,128)S(1)} custom-call(f32[4,2,3456]{2,1,0:T(2,128)} %dist_hbm.1, s32[2,4]{1,0:T(2,128)} %bitcast.11, f32[27,128]{1,0:T(8,128)} %bitcast.9, f32[27,128]{1,0:T(8,128)} %bitcast.10, s32[2,3456]{1,0:T(2,128)} %side_hbm.1, f32[2304,24]{1,0:T(8,128)} %bitcast.6, f32[2304,24]{1,0:T(8,128)} %bitcast.7, f32[576,24]{1,0:T(8,128)} %bitcast.8, ...), custom_call_target="tpu_custom_call" | custom-call | flops 3000000000 | bytes 10000000 | tf_op jit(solution)/shard_map/step/pallas_call | solution.py:610
  24.4 0.7 %spread.1 = f32[4,2,3456]{2,1,0:T(2,128)} custom-call(f32[216,128]{1,0:T(8,128)S(1)} %step.1.dense), custom_call_target="tpu_custom_call" | custom-call | tf_op jit(solution)/shard_map/spread/pallas_call | solution.py:622
